TPU v7x, 1024 devices: a whole 4x4x32 slice. The times are simulated.
1024 devices in a mesh: dp: 256 (over y, z, core), table: 4 (over x).
Axes of the slice: x: 4, y: 4, z: 32, core: 2. Of those that a mesh axis runs over, the one named last changes fastest.
Arguments:
- embeddings: bfloat16 [1024, 192, 512], P(('dp', 'table')), may hold values from -6 to 6
- lengths: int32 [1024], P(('dp', 'table')), may hold values from 16 to 192, as said below
- cotangent: bfloat16 [1024, 192, 512], P(('dp', 'table')), may hold values from -6 to 6
- w_proj: bfloat16 [512, 2048], replicated, may hold values from -0.25 to 0.25
- w_out: bfloat16 [512, 512], replicated, may hold values from -0.25 to 0.25
- routes: int32 [1024, 192, 1], P(('dp', 'table')), may hold values from 0 to 4; in each aligned block of 192 rows (0 to 191, 192 to 383, ..., all dimensions but the last counted through in order) at most 64 rows name the same one
- hot_ids: int32 [1024, 192], P(('dp', 'table')), may hold values from 0 to 1023
- cold_ids: int32 [1024, 192], P(('dp', 'table')), may hold values from 0 to 127
Outputs:
- hot_grad: float32 [1024, 512], P('dp')
- cold_grad: float32 [131072, 512], P(('dp', 'table'))
Inputs may be any that keep to these rules, and one draw needn't show every extreme that they name: `lengths`: every history has at least 16 valid items, and some history has 192. `routes`: among the 192 positions of one device, each of the values 0 to 4 appears at most 64 times.
All inputs are finite; a program needn't handle non-finite values.
Results may differ from a plain program's by a relative error of at most 0.015.
Values may be sent and summed in bfloat16 or wider, within the bound.
No kernel may reach another device: no remote copies, remote signals or barrier semaphores. Data moves between devices by JAX's collectives and lax.ppermute only.
A program may use at most 32 MiB of HBM per device.

v0:
```python
import jax
import jax.numpy as jnp
from jax import lax
from jax.sharding import PartitionSpec as P

HEAD_DIM = 64
HOT_DEV = 4
COLD_DEV = 128


epsilon = 1e-06


def layer_output(embedded, length, w_proj, w_out):
    seq_len = embedded.shape[0]
    model_width = embedded.shape[1]
    head_count = model_width // HEAD_DIM
    inputs = embedded.astype(jnp.float32)
    normed = (
        inputs * lax.rsqrt(jnp.mean(inputs * inputs, axis=-1, keepdims=True) + epsilon)
    ).astype(jnp.bfloat16)
    projected = jax.nn.silu(jnp.dot(normed, w_proj, preferred_element_type=jnp.float32)).astype(
        jnp.bfloat16
    )
    gate_part, value_part, query_part, key_part = jnp.split(projected, 4, axis=1)
    head_shape = (seq_len, head_count, HEAD_DIM)
    queries = query_part.reshape(head_shape).astype(jnp.float32)
    keys_all = key_part.reshape(head_shape).astype(jnp.float32)
    values_all = value_part.reshape(head_shape).astype(jnp.float32)
    scores = jnp.einsum("ihd,jhd->hij", queries, keys_all) * HEAD_DIM ** (-0.5)
    position = jnp.arange(seq_len)
    visible = (position[None, :] <= position[:, None]) & (position[:, None] < length)
    weights = (
        jnp.where(visible[None], jax.nn.silu(scores), 0.0) / length.astype(jnp.float32)
    ).astype(jnp.bfloat16)
    attended = jnp.einsum("hij,jhd->ihd", weights.astype(jnp.float32), values_all).reshape(
        seq_len, model_width
    )
    mixed = (
        attended
        * lax.rsqrt(jnp.mean(attended * attended, axis=-1, keepdims=True) + epsilon)
        * gate_part.astype(jnp.float32)
    ).astype(jnp.bfloat16)
    return inputs + jnp.dot(mixed, w_out, preferred_element_type=jnp.float32)


def item_gradient(embedded, length, cotangent, w_proj, w_out):

    def forward(embedded_in):
        return layer_output(embedded_in, length, w_proj, w_out)

    output, backward = jax.vjp(forward, embedded)
    (grad_rows,) = backward(cotangent.astype(output.dtype))
    position = jnp.arange(embedded.shape[0])
    return jnp.where((position < length)[:, None], grad_rows, jnp.zeros_like(grad_rows))


def shards(embeddings, lengths, cotangent, w_proj, w_out, routes, hot_ids, cold_ids):
    owners = lax.axis_size("table")

    def per_sequence(embedded, length, seq_cotangent):
        return item_gradient(embedded, length, seq_cotangent, w_proj, w_out)

    item_grad = jax.vmap(per_sequence)(embeddings, lengths, cotangent)
    row_total = item_grad.shape[0] * item_grad.shape[1]
    grad_rows = item_grad.reshape(row_total, item_grad.shape[2])
    route_flat = routes.reshape(row_total)
    hot_flat = hot_ids.reshape(row_total)
    cold_flat = cold_ids.reshape(row_total)
    is_hot = route_flat == owners
    bucket = jnp.arange(HOT_DEV * lax.axis_size("dp"))
    selector = ((hot_flat[None, :] == bucket[:, None]) & is_hot[None, :]).astype(jnp.bfloat16)
    local_share = lax.psum_scatter(
        jnp.dot(selector, grad_rows, preferred_element_type=jnp.float32),
        "dp",
        scatter_dimension=0,
        tiled=True,
    )
    hot_grad = lax.psum(local_share, "table")
    target = jnp.where(is_hot, 0, route_flat * COLD_DEV + cold_flat)
    cold_values = jnp.where(is_hot[:, None], 0.0, grad_rows.astype(jnp.float32))
    dense_sum = jax.ops.segment_sum(cold_values, target, num_segments=owners * COLD_DEV)
    cold_grad = lax.psum_scatter(dense_sum, "table", scatter_dimension=0, tiled=True)
    return (hot_grad, cold_grad)


def solution(mesh):
    return jax.shard_map(
        shards,
        mesh=mesh,
        in_specs=(
            P(("dp", "table"), None, None),
            P(("dp", "table")),
            P(("dp", "table"), None, None),
            P(),
            P(),
            P(("dp", "table"), None, None),
            P(("dp", "table"), None),
            P(("dp", "table"), None),
        ),
        out_specs=(P("dp", None), P(("dp", "table"), None)),
        check_vma=False,
    )
```

profile of v0, /device:TPU:24, one launch (start us, length us, event | category | flops | bytes accessed | tf_op | source)
XLA Modules:
  0.0 715.2 jit_solution(4646710666118144150)
XLA Ops:
  8.0 0.0 copy-start
  8.0 0.0 all-reduce.3.cloned.1.call-start
  8.9 1.0 fusion.33
  9.9 0.1 fusion.47
  10.0 0.0 copy-done
  10.0 1.6 fusion.39
  11.6 0.4 fusion.26
  12.0 0.8 fusion.52
  12.8 0.0 copy-done.1
  12.8 0.8 copy.32
  13.7 0.1 copy.34
  13.8 1.2 copy.33
  15.0 0.0 copy-start.12
  15.0 1.9 divide_convert_fusion
  17.0 0.0 copy-done.9
  17.0 0.9 copy-done.5
  17.8 0.4 fusion.27
  18.2 0.9 copy.37
  19.2 1.7 multiply_reduce_fusion
  20.9 0.7 copy-done.3
  21.6 0.8 add_add_fusion.1
  22.4 1.1 copy.38
  23.5 2.1 fusion.55
  25.6 2.5 fusion.7
  28.1 0.0 copy-start.15
  28.1 1.0 fusion.53
  29.1 1.1 fusion.54
  30.2 0.9 copy.35
  31.1 0.0 copy-done.4
  31.1 1.1 multiply_convert_fusion.1
  32.3 1.1 copy.39
  33.4 0.1 copy.40
  33.5 1.1 copy.41
  34.6 0.0 copy-done.6
  34.6 0.0 copy-start.13
  34.6 0.0 copy-start.14
  34.6 2.5 fusion.35
  37.2 0.2 fusion.42
  37.4 1.8 fusion.16
  39.2 0.0 all-reduce.3.cloned.1.call-update
  39.2 0.0 reduce-scatter.2.cloned.1.call-start
  39.2 0.6 copy-done.16
  39.8 2.8 scatter_custom_fusion
  42.6 0.0 reduce-scatter.2.cloned.1.call-update
  42.7 1.3 dynamic-slice
  44.6 651.3 %all-reduce.3.cloned.1.call-done = f32[1024,512]{1,0:T(8,128)} async-done(((f32[1024,512]{1,0:T(8,128)}), f32[1024,512]{1,0:T(8,128)}) %all-reduce.3.cloned.1.call-update) | async-done | bytes 2097168
  695.9 0.7 constant_dynamic-slice_fusion
  696.6 11.1 %psum.7 = f32[4,512]{1,0:T(4,128)} all-reduce(f32[4,512]{1,0:T(4,128)S(1)} %constant_dynamic-slice_fusion), channel_id=1, replica_groups=mesh['dp'=256,'table'=4] {'table'}, use_global_device_ids=true, to_apply=%region_5.6 | all-reduce | flops 2048 | bytes 16384 | tf_op jit(solution)/shard_map/psum | solution.py:79
  (28 shorter events, 0.1 us)
Async XLA Ops:
  8.0 2.0 copy-start
  8.0 687.9 %all-reduce.3.cloned.1.call-start = ((), (), s32[]{:S(2)}) async-start(), calls=%async_computation.2 | async-start | bytes 4194304
  11.6 1.2 copy-start.1
  13.8 3.1 copy-start.7
  15.0 2.0 copy-start.9
  15.0 2.8 copy-start.12
  17.0 0.9 copy-start.5
  19.2 2.4 copy-start.2
  20.9 0.8 copy-start.3
  25.6 2.5 copy-start.10
  25.6 3.5 copy-start.8
  28.1 2.1 copy-start.15
  28.1 3.1 copy-start.4
  30.2 4.4 copy-start.6
  31.1 2.2 copy-start.11
  34.6 2.6 copy-start.13
  34.6 2.8 copy-start.14
  39.2 0.7 copy-start.16
  39.2 668.5 %reduce-scatter.2.cloned.1.call-start = ((), (), s32[]{:S(2)}) async-start(), calls=%async_computation.1 | async-start | bytes 1310720 | tf_op jit(solution)/shard_map/reduce_scatter | solution.py:83
Sparse Core Ops, SparseCore 0:
  39.3 656.5 all-reduce.2
Sparse Core Ops, SparseCore 1:
  44.0 48.5 reduce-scatter.1
where the time goes:
time: 716 us; the launch traced here: 715 us
  waiting for transfers between devices  651 us (91%)
  between operations  17.2 us (2%)
  matrix products  16.5 us (2%)
  local copies, waits for them, and re-layouts  12.4 us (2%)
  blocking collectives  11.1 us (2%)
    unnamed x3, waiting for transfers between devices  651 us
  transfers between devices with their start and end apart: 2, of which 1 were waited for; matrix products, arithmetic and copies ran while one was open for 1% of the time, Pallas kernels for 0%

commit v1 on v0

v1 whole, which is shorter than its diff:
```python
import functools

import jax
import jax.numpy as jnp
from jax import lax
from jax.experimental import pallas as pl
from jax.experimental.pallas import tpu as pltpu
from jax.sharding import Mesh
from jax.sharding import PartitionSpec as P

HEAD_DIM = 64
HOT_DEV = 4
COLD_DEV = 128
CAP = 64
ID_ROWS = 16
ID_BASE = 32
PAIR = 2 * HEAD_DIM

epsilon = 1e-06
bf16 = jnp.bfloat16
f32 = jnp.float32


def dot(a, b, contract=((1,), (0,))):
    return lax.dot_general(a, b, (contract, ((), ())), preferred_element_type=f32)


def sigmoid(v):
    return 0.5 * jnp.tanh(0.5 * v) + 0.5


def item_kernel(owners, length_ref, emb_ref, cot_ref, w_proj_ref, w_out_ref, routes_ref, hot_ref, cold_ref, hot_out, cold_out, proj, slope, weight, factor, attended, heads_grad):
    seq, width = emb_ref.shape
    pairs = width // PAIR
    length = length_ref[0]

    x = emb_ref[...].astype(f32)
    root = lax.rsqrt(jnp.mean(x * x, axis=1, keepdims=True) + epsilon)
    xn = x * root
    normed = xn.astype(bf16)
    for part in range(4):
        cols = slice(part * width, (part + 1) * width)
        pre = dot(normed, w_proj_ref[:, cols])
        gate = sigmoid(pre)
        act = pre * gate
        slope[:, cols] = gate + act * (1.0 - gate)
        scale = HEAD_DIM ** (-0.5) if part == 2 else 1.0
        proj[:, cols] = (act.astype(bf16) * jnp.asarray(scale, bf16))

    rows = lax.broadcasted_iota(jnp.int32, (seq, seq), 0)
    lanes = lax.broadcasted_iota(jnp.int32, (seq, seq), 1)
    inverse = 1.0 / jnp.full((seq, seq), length, jnp.int32).astype(f32)
    mask = jnp.where((lanes <= rows) & (rows < length), inverse, 0.0)
    low = lax.broadcasted_iota(jnp.int32, (seq, PAIR), 1) < HEAD_DIM

    def split_heads(block):
        zero = jnp.zeros_like(block)
        return jnp.concatenate([jnp.where(low, block, zero), jnp.where(low, zero, block)], axis=0)

    def join_heads(block):
        return jnp.where(low, block[:seq], block[seq:])

    def part_of(part, pair):
        return proj[:, part * width + pair * PAIR : part * width + (pair + 1) * PAIR]

    for pair in range(pairs):
        scores = dot(split_heads(part_of(2, pair)), part_of(3, pair), ((1,), (1,)))
        for head in range(2):
            score = scores[head * seq : (head + 1) * seq]
            gate = sigmoid(score)
            act = score * gate
            weight[pair, head * seq : (head + 1) * seq, :] = (act * mask).astype(bf16)
            factor[pair, head * seq : (head + 1) * seq, :] = (gate + act * (1.0 - gate)) * mask
        attended[:, pair * PAIR : (pair + 1) * PAIR] = join_heads(dot(weight[pair], part_of(1, pair)))

    att = attended[...]
    att_root = lax.rsqrt(jnp.mean(att * att, axis=1, keepdims=True) + epsilon)
    att_n = att * att_root
    mixed_grad = dot(cot_ref[...], w_out_ref[...], ((1,), (1,))).astype(bf16).astype(f32)
    gate_part = proj[:, :width].astype(f32)
    gate_grad = (mixed_grad * att_n).astype(bf16).astype(f32)
    proj[:, :width] = (gate_grad * slope[:, :width]).astype(bf16)
    att_n_grad = mixed_grad * gate_part
    inner = jnp.mean(att_n_grad * att_n, axis=1, keepdims=True)
    heads_grad[...] = (att_root * (att_n_grad - att_n * inner)).astype(bf16)

    for pair in range(pairs):
        query, key, value = part_of(2, pair), part_of(3, pair), part_of(1, pair)
        grad_split = split_heads(heads_grad[:, pair * PAIR : (pair + 1) * PAIR])
        weight_grad = dot(grad_split, value, ((1,), (1,))).astype(bf16).astype(f32)
        score_grad = (weight_grad * factor[pair]).astype(bf16)
        value_grad = dot(weight[pair], grad_split, ((0,), (0,)))
        query_grad = join_heads(dot(score_grad, key)) * HEAD_DIM ** (-0.5)
        key_grad = dot(score_grad, split_heads(query), ((0,), (0,)))
        for part, grad in ((1, value_grad), (2, query_grad), (3, key_grad)):
            cols = slice(part * width + pair * PAIR, part * width + (pair + 1) * PAIR)
            proj[:, cols] = (grad.astype(bf16).astype(f32) * slope[:, cols]).astype(bf16)

    normed_grad = dot(proj[...], w_proj_ref[...], ((1,), (1,))).astype(bf16).astype(f32)
    inner = jnp.mean(normed_grad * xn, axis=1, keepdims=True)
    total = root * (normed_grad - xn * inner) + cot_ref[...].astype(f32)
    valid = lax.broadcasted_iota(jnp.int32, (seq, width), 0) < length
    grad_rows = jnp.where(valid, total, 0.0).astype(bf16)

    route = routes_ref[...]
    hot_id = hot_ref[...]
    is_hot = route == owners
    target = jnp.where(is_hot, -1, route * COLD_DEV + cold_ref[...])
    for owner in range(owners):
        bucket = lax.broadcasted_iota(jnp.int32, (COLD_DEV, seq), 0) + owner * COLD_DEV
        chosen = jnp.where(bucket == target, 1.0, 0.0).astype(bf16)
        cold_out[owner * COLD_DEV : (owner + 1) * COLD_DEV, :] = dot(chosen, grad_rows)

    before = jnp.where(rows < lanes, 1.0, 0.0).astype(bf16)
    hot_flag = jnp.where(is_hot, 1.0, 0.0)
    place = dot(hot_flag.astype(bf16), before).astype(jnp.int32)
    place = jnp.where(is_hot, place, -1)
    slots = lax.broadcasted_iota(jnp.int32, (CAP, seq), 0)
    chosen = jnp.where(slots == place, 1.0, 0.0).astype(bf16)
    hot_out[:CAP, :] = dot(chosen, grad_rows).astype(bf16)
    high = lax.shift_right_logical(hot_id, 5).astype(f32)
    rest = (hot_id & (ID_BASE - 1)).astype(f32)
    which = lax.broadcasted_iota(jnp.int32, (ID_ROWS, seq), 0)
    ids = jnp.where(which == 0, high, jnp.where(which == 1, rest, jnp.where(which == 2, 1.0, 0.0))).astype(bf16)
    slot_ids = dot(ids, chosen, ((1,), (1,)))
    hot_out[CAP:, :] = jnp.zeros((ID_ROWS, width), bf16)
    hot_out[CAP:, :PAIR] = jnp.concatenate([slot_ids, jnp.zeros((ID_ROWS, PAIR - CAP), f32)], axis=1).astype(bf16)


def item_call(owners, length, emb, cot, w_proj, w_out, routes, hot_ids, cold_ids):
    seq, width = emb.shape
    pairs = width // PAIR
    whole = pl.BlockSpec(memory_space=pltpu.VMEM)
    return pl.pallas_call(
        functools.partial(item_kernel, owners),
        in_specs=[pl.BlockSpec(memory_space=pltpu.SMEM)] + [whole] * 7,
        out_specs=[whole, whole],
        out_shape=[
            jax.ShapeDtypeStruct((CAP + ID_ROWS, width), bf16),
            jax.ShapeDtypeStruct((owners * COLD_DEV, width), f32),
        ],
        scratch_shapes=[
            pltpu.VMEM((seq, 4 * width), bf16),
            pltpu.VMEM((seq, 4 * width), f32),
            pltpu.VMEM((pairs, 2 * seq, seq), bf16),
            pltpu.VMEM((pairs, 2 * seq, seq), f32),
            pltpu.VMEM((seq, width), f32),
            pltpu.VMEM((seq, width), bf16),
        ],
        compiler_params=pltpu.CompilerParams(vmem_limit_bytes=48 * 1024 * 1024),
        cost_estimate=pl.CostEstimate(flops=1_200_000_000, bytes_accessed=4_500_000, transcendentals=700_000),
        name="item_grad",
    )(length, emb, cot, w_proj, w_out, routes, hot_ids, cold_ids)


def hot_kernel(z_size, cores, base_ref, rows_ref, out_ref):
    members = rows_ref.shape[0] // (CAP + ID_ROWS)
    buckets = z_size * HOT_DEV
    place = lax.broadcasted_iota(jnp.int32, (buckets, CAP), 0)
    bucket = (place // HOT_DEV) * (HOT_DEV * cores) + place % HOT_DEV + base_ref[0]
    total = jnp.zeros((buckets, rows_ref.shape[1]), f32)
    for member in range(members):
        start = member * (CAP + ID_ROWS)
        ids = rows_ref[start + CAP : start + CAP + ID_ROWS, :CAP].astype(f32)
        slot_id = ids[0:1] * ID_BASE + ids[1:2]
        slot_id = jnp.where(ids[2:3] > 0.5, slot_id, -1.0).astype(jnp.int32)
        chosen = jnp.where(bucket == slot_id, 1.0, 0.0).astype(bf16)
        total = total + dot(chosen, rows_ref[start : start + CAP, :])
    out_ref[...] = total.astype(bf16)


def hot_call(z_size, cores, base, rows):
    whole = pl.BlockSpec(memory_space=pltpu.VMEM)
    return pl.pallas_call(
        functools.partial(hot_kernel, z_size, cores),
        in_specs=[pl.BlockSpec(memory_space=pltpu.SMEM), whole],
        out_specs=whole,
        out_shape=jax.ShapeDtypeStruct((z_size * HOT_DEV, rows.shape[1]), bf16),
        cost_estimate=pl.CostEstimate(flops=80_000_000, bytes_accessed=800_000, transcendentals=0),
        name="hot_sum",
    )(base, rows)


def shards(embeddings, lengths, cotangent, w_proj, w_out, routes, hot_ids, cold_ids):
    owners = lax.axis_size("table")
    z_size, cores = lax.axis_size("z"), lax.axis_size("core")
    seq, width = embeddings.shape[1:]
    hot_rows, dense_cold = item_call(
        owners, lengths, embeddings.reshape(seq, width), cotangent.reshape(seq, width), w_proj, w_out,
        routes.reshape(1, seq), hot_ids, cold_ids,
    )
    cold_grad = lax.psum_scatter(dense_cold, "table", scatter_dimension=0, tiled=True)
    gathered = lax.all_gather(hot_rows, ("y", "core"), tiled=True)
    base = lax.axis_index("y") * (z_size * cores * HOT_DEV) + lax.axis_index("core") * HOT_DEV
    partial = hot_call(z_size, cores, base.reshape(1).astype(jnp.int32), gathered)
    parts = lax.all_to_all(partial.reshape(z_size, HOT_DEV, width), "z", 0, 0)
    share = jnp.sum(parts.astype(f32), axis=0)
    hot_grad = lax.psum(share, "table")
    return (hot_grad, cold_grad)


def solution(mesh):
    dp, table = mesh.devices.shape
    cores, y_size = 2, 4
    fine = Mesh(mesh.devices.reshape(y_size, dp // (y_size * cores), cores, table), ("y", "z", "core", "table"))
    every = ("y", "z", "core", "table")
    return jax.shard_map(
        shards,
        mesh=fine,
        in_specs=(
            P(every, None, None),
            P(every),
            P(every, None, None),
            P(),
            P(),
            P(every, None, None),
            P(every, None),
            P(every, None),
        ),
        out_specs=(P(("y", "z", "core"), None), P(every, None)),
        check_vma=False,
    )
```

time: 716 us -> 116 us (0.16)
  waiting for transfers between devices: 651 us -> 0.02 us
  blocking collectives: 11.1 us -> 86 us
  matrix products: 16.5 us -> 0 us
  Pallas kernels: 0 us -> 7.52 us
    unnamed x3 -> x1, waiting for transfers between devices: 651 us -> 0.02 us
    all_to_all x0 -> x1, blocking collectives: none -> 50.6 us  [shards(): parts = lax.all_to_all(partial.reshape(z_size, HOT_DEV, width), 'z', 0, 0)]
    all_gather x0 -> x1, blocking collectives: none -> 24.2 us  [shards(): gathered = lax.all_gather(hot_rows, ('y', 'core'), tiled=True)]
    dot_general x10 -> x0, matrix products: 16.5 us -> none  [the longest x3 4.95 us: layer_output(): jnp.einsum('hij,jhd->ihd', weights.astype(jnp.float32), values_all)]
    pallas_call x0 -> x2, Pallas kernels: none -> 7.52 us  [the longest x1 5.36 us: item_call(): pl.pallas_call(functools.partial(item_kernel, owners), in_specs=[pl.Block...]
  transfers between devices with their start and end apart: 2 -> 1, of which waited for: 1 -> 0; matrix products, arithmetic and copies ran while one was open for 1% -> 1% of each run, Pallas kernels for 0% -> 2%
where the time goes in v1:
time: 116 us
  blocking collectives  86 us (74%)
  between operations  14.7 us (13%)
  Pallas kernels  7.52 us (6%)
  local copies, waits for them, and re-layouts  7.45 us (6%)
    all_to_all x1, blocking collectives, shards(): parts = lax.all_to_all(partial.reshape(z_size, HOT_DEV, width), 'z', 0, 0)  50.6 us
    all_gather x1, blocking collectives, shards(): gathered = lax.all_gather(hot_rows, ('y', 'core'), tiled=True)  24.2 us
    psum x1, blocking collectives, shards(): hot_grad = lax.psum(share, 'table')  11.2 us
    unnamed x14, local copies, waits for them, and re-layouts  6.51 us
    pallas_call x1, Pallas kernels, item_call(): pl.pallas_call(functools.partial(item_kernel, owners), in_specs=[pl.Block...  5.36 us
  transfers between devices with their start and end apart: 1, of which 0 were waited for; matrix products, arithmetic and copies ran while one was open for 1% of the time, Pallas kernels for 2%

profile of v1, /device:TPU:24, one launch (start us, length us, event | category | flops | bytes accessed | tf_op | source)
XLA Modules:
  0.0 115.8 jit_solution(105484491584399774)
XLA Ops:
  7.2 0.0 reduce-scatter.2.cloned.1.call-start
  7.9 0.0 copy-start
  7.9 1.6 %copy-done = bf16[512,2048]{1,0:T(8,128)(2,1)S(1)} copy-done((bf16[512,2048]{1,0:T(8,128)(2,1)S(1)}, bf16[512,2048]{1,0:T(8,128)(2,1)}, u32[]{:S(2)}) %copy-start) | copy-done | bytes 2097176
  9.4 0.0 copy-start.1
  9.5 1.0 copy-done.1
  10.5 0.0 copy-start.2
  10.5 0.9 copy-done.2
  11.4 0.0 copy-start.3
  11.4 0.9 copy-done.3
  12.3 0.0 copy-start.4
  12.3 0.7 copy-done.4
  13.0 0.0 copy-start.5
  13.0 0.7 copy-done.5
  13.7 0.0 copy-start.6
  13.7 0.7 copy-done.6
  14.4 5.4 %item_grad.1 = (bf16[80,512]{1,0:T(8,128)(2,1)S(1)}, f32[512,512]{1,0:T(8,128)}) custom-call(s32[1]{0:T(128)S(6)} %copy.10.length_ref, bf16[192,512]{1,0:T(8,128)(2,1)S(1)} %bitcast.4, bf16[192,512]{1,0:T(8,128)(2,1)S(1)} %bitcast.5, bf16[512,2048]{1,0:T(8,128)(2,1)S(1)} %copy-done, bf16[512,512]{1,0:T(8,128)(2,1)S(1)} %copy-done.1, s32[1,192]{1,0:T(1,128)S(1)} %bitcast.6, ...), custom_call_target="tpu_custom_call" | custom-call | flops 1200000000 | bytes 4500000 | tf_op jit(solution)/shard_map/item_grad/pallas_call | solution.py:134
  19.7 0.0 reduce-scatter.2.cloned.1.call-update
  19.8 24.2 %all_gather.3.rows_ref = bf16[640,512]{1,0:T(8,128)(2,1)} all-gather(bf16[80,512]{1,0:T(8,128)(2,1)S(1)} %get-tuple-element.4), channel_id=1, replica_groups=mesh['y'=4,'z'=32,'core'=2,'table'=4] {'y','core'}, dimensions={0}, use_global_device_ids=true | all-gather | bytes 737280 | tf_op jit(solution)/shard_map/all_gather | solution.py:193
  44.0 2.2 %hot_sum.1 = bf16[128,512]{1,0:T(8,128)(2,1)} custom-call(s32[1]{0:T(128)} %bitcast.base_ref, bf16[640,512]{1,0:T(8,128)(2,1)} %all_gather.3.rows_ref), custom_call_target="tpu_custom_call" | custom-call | flops 80000000 | bytes 800000 | tf_op jit(solution)/shard_map/hot_sum/pallas_call | solution.py:174
  46.2 0.9 reshape.23
  47.1 50.6 %all_to_all.5 = bf16[32,4,512]{2,1,0:T(4,128)(2,1)S(1)} all-to-all(bf16[32,4,512]{2,1,0:T(4,128)(2,1)S(1)} %reshape.23), channel_id=1, replica_groups=mesh['y'=4,'z'=32,'core'=2,'table'=4] {'z'}, dimensions={0} | all-to-all | bytes 262144 | tf_op jit(solution)/shard_map/all_to_all | solution.py:196
  97.7 0.1 convert_reduce_fusion
  97.8 11.2 %psum.7 = f32[4,512]{1,0:T(4,128)} all-reduce(f32[4,512]{1,0:T(4,128)S(1)} %convert_reduce_fusion), channel_id=1, replica_groups=mesh['y'=4,'z'=32,'core'=2,'table'=4] {'table'}, use_global_device_ids=true, to_apply=%region_1.0 | all-reduce | flops 2048 | bytes 16384 | tf_op jit(solution)/shard_map/psum | solution.py:198
  109.0 0.0 reduce-scatter.2.cloned.1.call-done
Async XLA Ops:
  7.2 101.8 %reduce-scatter.2.cloned.1.call-start = ((), (), s32[]{:S(2)}) async-start(), calls=%async_computation.2 | async-start | bytes 1310720 | tf_op jit(solution)/shard_map/reduce_scatter | solution.py:192
  7.9 1.6 %copy-start = (bf16[512,2048]{1,0:T(8,128)(2,1)S(1)}, bf16[512,2048]{1,0:T(8,128)(2,1)}, u32[]{:S(2)}) copy-start(bf16[512,2048]{1,0:T(8,128)(2,1)} %w_proj_ref.1) | copy-start | bytes 6291460
  9.4 1.0 copy-start.1
  10.5 0.9 copy-start.2
  11.4 0.9 copy-start.3
  12.3 0.7 copy-start.4
  13.0 0.7 copy-start.5
  13.7 0.7 copy-start.6
Sparse Core Ops, SparseCore 0:
  19.9 48.6 reduce-scatter.1

commit v2 on v1

--- a/solution.py
+++ b/solution.py
@@ -29,17 +29,32 @@
     return 0.5 * jnp.tanh(0.5 * v) + 0.5
 
 
-def item_kernel(owners, length_ref, emb_ref, cot_ref, w_proj_ref, w_out_ref, routes_ref, hot_ref, cold_ref, hot_out, cold_out, proj, slope, weight, factor, attended, heads_grad):
+def item_kernel(owners, *refs):
+    length_ref, emb_hbm, cot_hbm, w_proj_hbm, w_out_hbm, routes_hbm, hot_hbm, cold_hbm = refs[:8]
+    hot_out, cold_out = refs[8:10]
+    emb_ref, cot_ref, w_proj_ref, w_out_ref, routes_ref, hot_ref, cold_ref = refs[10:17]
+    proj, slope, weight, factor, attended, heads_grad, sems = refs[17:]
     seq, width = emb_ref.shape
     pairs = width // PAIR
     length = length_ref[0]
 
+    loads = [(emb_hbm, emb_ref)]
+    for part in (2, 3, 1, 0):
+        cols = pl.ds(part * width, width)
+        loads.append((w_proj_hbm.at[:, cols], w_proj_ref.at[:, cols]))
+    loads += [(cot_hbm, cot_ref), (w_out_hbm, w_out_ref), (routes_hbm, routes_ref), (hot_hbm, hot_ref), (cold_hbm, cold_ref)]
+    loads = [pltpu.make_async_copy(src, dst, sems.at[i]) for i, (src, dst) in enumerate(loads)]
+    for load in loads:
+        load.start()
+
+    loads[0].wait()
     x = emb_ref[...].astype(f32)
     root = lax.rsqrt(jnp.mean(x * x, axis=1, keepdims=True) + epsilon)
     xn = x * root
     normed = xn.astype(bf16)
-    for part in range(4):
+    for step, part in enumerate((2, 3, 1, 0)):
         cols = slice(part * width, (part + 1) * width)
+        loads[1 + step].wait()
         pre = dot(normed, w_proj_ref[:, cols])
         gate = sigmoid(pre)
         act = pre * gate
@@ -73,6 +88,8 @@
             factor[pair, head * seq : (head + 1) * seq, :] = (gate + act * (1.0 - gate)) * mask
         attended[:, pair * PAIR : (pair + 1) * PAIR] = join_heads(dot(weight[pair], part_of(1, pair)))
 
+    loads[5].wait()
+    loads[6].wait()
     att = attended[...]
     att_root = lax.rsqrt(jnp.mean(att * att, axis=1, keepdims=True) + epsilon)
     att_n = att * att_root
@@ -102,98 +119,122 @@
     valid = lax.broadcasted_iota(jnp.int32, (seq, width), 0) < length
     grad_rows = jnp.where(valid, total, 0.0).astype(bf16)
 
+    for load in loads[7:]:
+        load.wait()
     route = routes_ref[...]
-    hot_id = hot_ref[...]
-    is_hot = route == owners
-    target = jnp.where(is_hot, -1, route * COLD_DEV + cold_ref[...])
-    for owner in range(owners):
-        bucket = lax.broadcasted_iota(jnp.int32, (COLD_DEV, seq), 0) + owner * COLD_DEV
-        chosen = jnp.where(bucket == target, 1.0, 0.0).astype(bf16)
-        cold_out[owner * COLD_DEV : (owner + 1) * COLD_DEV, :] = dot(chosen, grad_rows)
-
+    bucket = jnp.where(route == owners, hot_ref[...], cold_ref[...])
+    kind = lax.broadcasted_iota(jnp.int32, (ID_ROWS, seq), 0)
+    named = kind == route
     before = jnp.where(rows < lanes, 1.0, 0.0).astype(bf16)
-    hot_flag = jnp.where(is_hot, 1.0, 0.0)
-    place = dot(hot_flag.astype(bf16), before).astype(jnp.int32)
-    place = jnp.where(is_hot, place, -1)
+    place = dot(jnp.where(named, 1.0, 0.0).astype(bf16), before).astype(jnp.int32)
+    place = jnp.where(named, place, -1)
+    high = lax.shift_right_logical(bucket, 5).astype(f32)
+    rest = (bucket & (ID_BASE - 1)).astype(f32)
+    ids = jnp.where(kind == 0, high, jnp.where(kind == 1, rest, jnp.where(kind == 2, 1.0, 0.0))).astype(bf16)
     slots = lax.broadcasted_iota(jnp.int32, (CAP, seq), 0)
-    chosen = jnp.where(slots == place, 1.0, 0.0).astype(bf16)
-    hot_out[:CAP, :] = dot(chosen, grad_rows).astype(bf16)
-    high = lax.shift_right_logical(hot_id, 5).astype(f32)
-    rest = (hot_id & (ID_BASE - 1)).astype(f32)
-    which = lax.broadcasted_iota(jnp.int32, (ID_ROWS, seq), 0)
-    ids = jnp.where(which == 0, high, jnp.where(which == 1, rest, jnp.where(which == 2, 1.0, 0.0))).astype(bf16)
-    slot_ids = dot(ids, chosen, ((1,), (1,)))
-    hot_out[CAP:, :] = jnp.zeros((ID_ROWS, width), bf16)
-    hot_out[CAP:, :PAIR] = jnp.concatenate([slot_ids, jnp.zeros((ID_ROWS, PAIR - CAP), f32)], axis=1).astype(bf16)
+    for owner in range(owners + 1):
+        out = hot_out if owner == owners else cold_out.at[owner]
+        chosen = jnp.where(slots == place[owner : owner + 1], 1.0, 0.0).astype(bf16)
+        out[:CAP, :] = dot(chosen, grad_rows).astype(bf16)
+        slot_ids = dot(ids, chosen, ((1,), (1,)))
+        out[CAP:, :] = jnp.zeros((ID_ROWS, width), bf16)
+        out[CAP:, :PAIR] = jnp.concatenate([slot_ids, jnp.zeros((ID_ROWS, PAIR - CAP), f32)], axis=1).astype(bf16)
 
 
 def item_call(owners, length, emb, cot, w_proj, w_out, routes, hot_ids, cold_ids):
     seq, width = emb.shape
     pairs = width // PAIR
     whole = pl.BlockSpec(memory_space=pltpu.VMEM)
+    loaded = (emb, cot, w_proj, w_out, routes, hot_ids, cold_ids)
     return pl.pallas_call(
         functools.partial(item_kernel, owners),
-        in_specs=[pl.BlockSpec(memory_space=pltpu.SMEM)] + [whole] * 7,
+        in_specs=[pl.BlockSpec(memory_space=pltpu.SMEM)] + [pl.BlockSpec(memory_space=pltpu.HBM)] * 7,
         out_specs=[whole, whole],
         out_shape=[
             jax.ShapeDtypeStruct((CAP + ID_ROWS, width), bf16),
-            jax.ShapeDtypeStruct((owners * COLD_DEV, width), f32),
+            jax.ShapeDtypeStruct((owners, CAP + ID_ROWS, width), bf16),
         ],
-        scratch_shapes=[
+        scratch_shapes=[pltpu.VMEM(a.shape, a.dtype) for a in loaded]
+        + [
             pltpu.VMEM((seq, 4 * width), bf16),
             pltpu.VMEM((seq, 4 * width), f32),
             pltpu.VMEM((pairs, 2 * seq, seq), bf16),
             pltpu.VMEM((pairs, 2 * seq, seq), f32),
             pltpu.VMEM((seq, width), f32),
             pltpu.VMEM((seq, width), bf16),
+            pltpu.SemaphoreType.DMA((10,)),
         ],
-        compiler_params=pltpu.CompilerParams(vmem_limit_bytes=48 * 1024 * 1024),
+        compiler_params=pltpu.CompilerParams(vmem_limit_bytes=64 * 1024 * 1024),
         cost_estimate=pl.CostEstimate(flops=1_200_000_000, bytes_accessed=4_500_000, transcendentals=700_000),
         name="item_grad",
-    )(length, emb, cot, w_proj, w_out, routes, hot_ids, cold_ids)
-
-
-def hot_kernel(z_size, cores, base_ref, rows_ref, out_ref):
-    members = rows_ref.shape[0] // (CAP + ID_ROWS)
-    buckets = z_size * HOT_DEV
-    place = lax.broadcasted_iota(jnp.int32, (buckets, CAP), 0)
-    bucket = (place // HOT_DEV) * (HOT_DEV * cores) + place % HOT_DEV + base_ref[0]
-    total = jnp.zeros((buckets, rows_ref.shape[1]), f32)
-    for member in range(members):
-        start = member * (CAP + ID_ROWS)
-        ids = rows_ref[start + CAP : start + CAP + ID_ROWS, :CAP].astype(f32)
+    )(length, *loaded)
+
+
+def sum_rows(rows_ref, bucket):
+    total = jnp.zeros((bucket.shape[0], rows_ref.shape[2]), f32)
+    for member in range(rows_ref.shape[0]):
+        ids = rows_ref[member, CAP:, :CAP].astype(f32)
         slot_id = ids[0:1] * ID_BASE + ids[1:2]
         slot_id = jnp.where(ids[2:3] > 0.5, slot_id, -1.0).astype(jnp.int32)
         chosen = jnp.where(bucket == slot_id, 1.0, 0.0).astype(bf16)
-        total = total + dot(chosen, rows_ref[start : start + CAP, :])
-    out_ref[...] = total.astype(bf16)
-
-
-def hot_call(z_size, cores, base, rows):
+        total = total + dot(chosen, rows_ref[member, :CAP, :])
+    return total
+
+
+def hot_kernel(cores, first, base_ref, rows_ref, out_ref):
+    z_size = out_ref.shape[0]
+    place = lax.broadcasted_iota(jnp.int32, (z_size * HOT_DEV, CAP), 0)
+    z = place // HOT_DEV + first
+    z = jnp.where(z >= z_size, z - z_size, z)
+    bucket = z * (HOT_DEV * cores) + place % HOT_DEV + base_ref[0]
+    out_ref[...] = sum_rows(rows_ref, bucket).reshape(out_ref.shape).astype(bf16)
+
+
+def hot_call(z_size, cores, first, base, rows):
     whole = pl.BlockSpec(memory_space=pltpu.VMEM)
     return pl.pallas_call(
-        functools.partial(hot_kernel, z_size, cores),
+        functools.partial(hot_kernel, cores, first),
         in_specs=[pl.BlockSpec(memory_space=pltpu.SMEM), whole],
         out_specs=whole,
-        out_shape=jax.ShapeDtypeStruct((z_size * HOT_DEV, rows.shape[1]), bf16),
+        out_shape=jax.ShapeDtypeStruct((z_size, HOT_DEV, rows.shape[2]), bf16),
+        compiler_params=pltpu.CompilerParams(vmem_limit_bytes=16 * 1024 * 1024),
         cost_estimate=pl.CostEstimate(flops=80_000_000, bytes_accessed=800_000, transcendentals=0),
         name="hot_sum",
     )(base, rows)
+
+
+def cold_kernel(rows_ref, out_ref):
+    out_ref[...] = sum_rows(rows_ref, lax.broadcasted_iota(jnp.int32, (COLD_DEV, CAP), 0))
+
+
+def cold_call(rows):
+    whole = pl.BlockSpec(memory_space=pltpu.VMEM)
+    return pl.pallas_call(
+        cold_kernel,
+        in_specs=[whole],
+        out_specs=whole,
+        out_shape=jax.ShapeDtypeStruct((COLD_DEV, rows.shape[2]), f32),
+        compiler_params=pltpu.CompilerParams(vmem_limit_bytes=16 * 1024 * 1024),
+        cost_estimate=pl.CostEstimate(flops=40_000_000, bytes_accessed=600_000, transcendentals=0),
+        name="cold_sum",
+    )(rows)
 
 
 def shards(embeddings, lengths, cotangent, w_proj, w_out, routes, hot_ids, cold_ids):
     owners = lax.axis_size("table")
     z_size, cores = lax.axis_size("z"), lax.axis_size("core")
     seq, width = embeddings.shape[1:]
-    hot_rows, dense_cold = item_call(
+    hot_rows, cold_rows = item_call(
         owners, lengths, embeddings.reshape(seq, width), cotangent.reshape(seq, width), w_proj, w_out,
         routes.reshape(1, seq), hot_ids, cold_ids,
     )
-    cold_grad = lax.psum_scatter(dense_cold, "table", scatter_dimension=0, tiled=True)
-    gathered = lax.all_gather(hot_rows, ("y", "core"), tiled=True)
+    cold_grad = cold_call(lax.all_to_all(cold_rows, "table", 0, 0))
+    gathered = lax.all_gather(hot_rows, ("y", "core"))
     base = lax.axis_index("y") * (z_size * cores * HOT_DEV) + lax.axis_index("core") * HOT_DEV
-    partial = hot_call(z_size, cores, base.reshape(1).astype(jnp.int32), gathered)
-    parts = lax.all_to_all(partial.reshape(z_size, HOT_DEV, width), "z", 0, 0)
+    first = z_size * 5 // 8
+    order = [(first + i) % z_size for i in range(z_size)]
+    partial = hot_call(z_size, cores, first, base.reshape(1).astype(jnp.int32), gathered)
+    parts = lax.all_to_all(partial, "z", 0, 0, axis_index_groups=[order])
     share = jnp.sum(parts.astype(f32), axis=0)
     hot_grad = lax.psum(share, "table")
     return (hot_grad, cold_grad)

time: 116 us -> 87.3 us (0.75)
  blocking collectives: 86 us -> 34.4 us
  starting transfers between devices: 0.04 us -> 26 us
  waiting for transfers between devices: 0.02 us -> 15.8 us
  between operations: 14.7 us -> 1.3 us
  local copies, waits for them, and re-layouts: 7.45 us -> 0 us
  Pallas kernels: 7.52 us -> 9.2 us
    all_to_all x1 -> x0, blocking collectives: 50.6 us -> none  [shards(): parts = lax.all_to_all(partial.reshape(z_size, HOT_DEV, width), 'z', 0, 0)]
    all_to_all x0 -> x2, starting transfers between devices: none -> 26 us  [the longest x1 21.7 us: shards(): parts = lax.all_to_all(partial, 'z', 0, 0, axis_index_groups=[order])]
    all_to_all x0 -> x2, waiting for transfers between devices: none -> 15.8 us  [the longest x1 15.8 us: shards(): parts = lax.all_to_all(partial, 'z', 0, 0, axis_index_groups=[order])]
    unnamed x14 -> x0, local copies, waits for them, and re-layouts: 6.51 us -> none
    pallas_call x1, Pallas kernels: 5.36 us -> 7.12 us  [item_call(): pl.pallas_call(functools.partial(item_kernel, owners), in_specs=[pl.Block...]
    all_gather x1, blocking collectives: 24.2 us -> 22.8 us  [shards(): gathered = lax.all_gather(hot_rows, ('y', 'core'))]
  transfers between devices with their start and end apart: 1 -> 2, of which waited for: 0 -> 1; matrix products, arithmetic and copies ran while one was open for 1% -> 0% of each run, Pallas kernels for 2% -> 2%
where the time goes in v2:
time: 87.3 us; the launch traced here: 86.8 us
  blocking collectives  34.4 us (39%)
  starting transfers between devices  26 us (30%)
  waiting for transfers between devices  15.8 us (18%)
  Pallas kernels  9.2 us (11%)
  between operations  1.3 us (1%)
    all_gather x1, blocking collectives, shards(): gathered = lax.all_gather(hot_rows, ('y', 'core'))  22.8 us
    all_to_all x1, starting transfers between devices, shards(): parts = lax.all_to_all(partial, 'z', 0, 0, axis_index_groups=[order])  21.7 us
    all_to_all x1, waiting for transfers between devices, shards(): parts = lax.all_to_all(partial, 'z', 0, 0, axis_index_groups=[order])  15.8 us
    psum x1, blocking collectives, shards(): hot_grad = lax.psum(share, 'table')  11.6 us
    pallas_call x1, Pallas kernels, item_call(): pl.pallas_call(functools.partial(item_kernel, owners), in_specs=[pl.Block...  7.12 us
    all_to_all x1, starting transfers between devices, shards(): cold_grad = cold_call(lax.all_to_all(cold_rows, 'table', 0, 0))  4.29 us
  transfers between devices with their start and end apart: 2, of which 1 were waited for; matrix products, arithmetic and copies ran while one was open for 0% of the time, Pallas kernels for 2%

profile of v2, /device:TPU:24, one launch (start us, length us, event | category | flops | bytes accessed | tf_op | source)
XLA Modules:
  0.0 86.8 jit_solution(13942268260051097636)
XLA Ops:
  1.3 7.1 %item_grad.1 = (bf16[80,512]{1,0:T(8,128)(2,1)}, bf16[4,80,512]{2,1,0:T(8,128)(2,1)}) custom-call(s32[1]{0:T(128)S(6)} %copy.10.refs_0_, bf16[192,512]{1,0:T(8,128)(2,1)} %bitcast.6, bf16[192,512]{1,0:T(8,128)(2,1)} %bitcast.7, bf16[512,2048]{1,0:T(8,128)(2,1)} %refs_3_.1, bf16[512,512]{1,0:T(8,128)(2,1)} %refs_4_.1, s32[1,192]{1,0:T(1,128)} %bitcast.8, ...), custom_call_target="tpu_custom_call" | custom-call | flops 1200000000 | bytes 4500000 | tf_op jit(solution)/shard_map/item_grad/pallas_call | solution.py:149
  8.4 4.3 %all-to-all-start.1 = ((bf16[4,80,512]{2,1,0:T(8,128)(2,1)}), bf16[4,80,512]{2,1,0:T(8,128)(2,1)S(1)}, u32[]{:S(2)}, u32[]{:S(2)}) async-start(bf16[4,80,512]{2,1,0:T(8,128)(2,1)} %get-tuple-element.5), calls=%async_computation.1 | async-start | bytes 655360 | tf_op jit(solution)/shard_map/all_to_all | solution.py:231
  12.7 22.8 %all-gather = bf16[640,512]{1,0:T(8,128)(2,1)S(1)} all-gather(bf16[80,512]{1,0:T(8,128)(2,1)} %get-tuple-element.4), channel_id=2, replica_groups=mesh['y'=4,'z'=32,'core'=2,'table'=4] {'y','core'}, dimensions={0}, use_global_device_ids=true | all-gather | bytes 737280 | tf_op jit(solution)/shard_map/all_gather | solution.py:232
  35.5 1.1 %hot_sum.1 = bf16[32,4,512]{2,1,0:T(4,128)(2,1)} custom-call(s32[1]{0:T(128)} %bitcast.base_ref, bf16[8,80,512]{2,1,0:T(8,128)(2,1)S(1)} %bitcast.5), custom_call_target="tpu_custom_call" | custom-call | flops 80000000 | bytes 800000 | tf_op jit(solution)/shard_map/hot_sum/pallas_call | solution.py:195
  36.6 0.0 all-to-all-done.1.rows_ref
  36.6 21.7 %all-to-all-start = ((bf16[32,4,512]{2,1,0:T(4,128)(2,1)}), bf16[32,4,512]{2,1,0:T(4,128)(2,1)S(1)}, u32[]{:S(2)}, u32[]{:S(2)}) async-start(bf16[32,4,512]{2,1,0:T(4,128)(2,1)} %hot_sum.1), calls=%async_computation | async-start | bytes 262144 | tf_op jit(solution)/shard_map/all_to_all | solution.py:237
  58.3 1.0 %cold_sum.1 = f32[128,512]{1,0:T(8,128)} custom-call(bf16[4,80,512]{2,1,0:T(8,128)(2,1)S(1)} %all-to-all-done.1.rows_ref), custom_call_target="tpu_custom_call" | custom-call | flops 40000000 | bytes 600000 | tf_op jit(solution)/shard_map/cold_sum/pallas_call | solution.py:212
  59.3 15.8 %all-to-all-done = bf16[32,4,512]{2,1,0:T(4,128)(2,1)S(1)} async-done(((bf16[32,4,512]{2,1,0:T(4,128)(2,1)}), bf16[32,4,512]{2,1,0:T(4,128)(2,1)S(1)}, u32[]{:S(2)}, u32[]{:S(2)}) %all-to-all-start) | async-done | bytes 131104 | tf_op jit(solution)/shard_map/all_to_all | solution.py:237
  75.1 0.1 convert_reduce_fusion
  75.1 11.6 %psum.7 = f32[4,512]{1,0:T(4,128)} all-reduce(f32[4,512]{1,0:T(4,128)S(1)} %convert_reduce_fusion), channel_id=1, replica_groups=mesh['y'=4,'z'=32,'core'=2,'table'=4] {'table'}, use_global_device_ids=true, to_apply=%region_1.0 | all-reduce | flops 2048 | bytes 16384 | tf_op jit(solution)/shard_map/psum | solution.py:239
Async XLA Ops:
  8.4 28.2 %all-to-all-start.1 = ((bf16[4,80,512]{2,1,0:T(8,128)(2,1)}), bf16[4,80,512]{2,1,0:T(8,128)(2,1)S(1)}, u32[]{:S(2)}, u32[]{:S(2)}) async-start(bf16[4,80,512]{2,1,0:T(8,128)(2,1)} %get-tuple-element.5), calls=%async_computation.1 | async-start | bytes 655360 | tf_op jit(solution)/shard_map/all_to_all | solution.py:231
  36.6 38.5 %all-to-all-start = ((bf16[32,4,512]{2,1,0:T(4,128)(2,1)}), bf16[32,4,512]{2,1,0:T(4,128)(2,1)S(1)}, u32[]{:S(2)}, u32[]{:S(2)}) async-start(bf16[32,4,512]{2,1,0:T(4,128)(2,1)} %hot_sum.1), calls=%async_computation | async-start | bytes 262144 | tf_op jit(solution)/shard_map/all_to_all | solution.py:237

commit v3 on v2

--- a/solution.py
+++ b/solution.py
@@ -30,10 +30,10 @@
 
 
 def item_kernel(owners, *refs):
-    length_ref, emb_hbm, cot_hbm, w_proj_hbm, w_out_hbm, routes_hbm, hot_hbm, cold_hbm = refs[:8]
-    hot_out, cold_out = refs[8:10]
-    emb_ref, cot_ref, w_proj_ref, w_out_ref, routes_ref, hot_ref, cold_ref = refs[10:17]
-    proj, slope, weight, factor, attended, heads_grad, sems = refs[17:]
+    length_ref, me_ref, emb_hbm, cot_hbm, w_proj_hbm, w_out_hbm, routes_hbm, hot_hbm, cold_hbm = refs[:9]
+    outs = refs[9 : 10 + owners]
+    emb_ref, cot_ref, w_proj_ref, w_out_ref, routes_ref, hot_ref, cold_ref = refs[10 + owners : 17 + owners]
+    proj, slope, weight, factor, attended, heads_grad, sems = refs[17 + owners :]
     seq, width = emb_ref.shape
     pairs = width // PAIR
     length = length_ref[0]
@@ -124,7 +124,9 @@
     route = routes_ref[...]
     bucket = jnp.where(route == owners, hot_ref[...], cold_ref[...])
     kind = lax.broadcasted_iota(jnp.int32, (ID_ROWS, seq), 0)
-    named = kind == route
+    shift = route - me_ref[0]
+    shift = jnp.where(route == owners, owners, jnp.where(shift < 0, shift + owners, shift))
+    named = kind == shift
     before = jnp.where(rows < lanes, 1.0, 0.0).astype(bf16)
     place = dot(jnp.where(named, 1.0, 0.0).astype(bf16), before).astype(jnp.int32)
     place = jnp.where(named, place, -1)
@@ -132,28 +134,24 @@
     rest = (bucket & (ID_BASE - 1)).astype(f32)
     ids = jnp.where(kind == 0, high, jnp.where(kind == 1, rest, jnp.where(kind == 2, 1.0, 0.0))).astype(bf16)
     slots = lax.broadcasted_iota(jnp.int32, (CAP, seq), 0)
-    for owner in range(owners + 1):
-        out = hot_out if owner == owners else cold_out.at[owner]
-        chosen = jnp.where(slots == place[owner : owner + 1], 1.0, 0.0).astype(bf16)
+    for step, out in enumerate(outs):
+        chosen = jnp.where(slots == place[step : step + 1], 1.0, 0.0).astype(bf16)
         out[:CAP, :] = dot(chosen, grad_rows).astype(bf16)
         slot_ids = dot(ids, chosen, ((1,), (1,)))
         out[CAP:, :] = jnp.zeros((ID_ROWS, width), bf16)
         out[CAP:, :PAIR] = jnp.concatenate([slot_ids, jnp.zeros((ID_ROWS, PAIR - CAP), f32)], axis=1).astype(bf16)
 
 
-def item_call(owners, length, emb, cot, w_proj, w_out, routes, hot_ids, cold_ids):
+def item_call(owners, length, me, emb, cot, w_proj, w_out, routes, hot_ids, cold_ids):
     seq, width = emb.shape
     pairs = width // PAIR
     whole = pl.BlockSpec(memory_space=pltpu.VMEM)
     loaded = (emb, cot, w_proj, w_out, routes, hot_ids, cold_ids)
     return pl.pallas_call(
         functools.partial(item_kernel, owners),
-        in_specs=[pl.BlockSpec(memory_space=pltpu.SMEM)] + [pl.BlockSpec(memory_space=pltpu.HBM)] * 7,
-        out_specs=[whole, whole],
-        out_shape=[
-            jax.ShapeDtypeStruct((CAP + ID_ROWS, width), bf16),
-            jax.ShapeDtypeStruct((owners, CAP + ID_ROWS, width), bf16),
-        ],
+        in_specs=[pl.BlockSpec(memory_space=pltpu.SMEM)] * 2 + [pl.BlockSpec(memory_space=pltpu.HBM)] * 7,
+        out_specs=[whole] * (owners + 1),
+        out_shape=[jax.ShapeDtypeStruct((CAP + ID_ROWS, width), bf16)] * (owners + 1),
         scratch_shapes=[pltpu.VMEM(a.shape, a.dtype) for a in loaded]
         + [
             pltpu.VMEM((seq, 4 * width), bf16),
@@ -167,17 +165,17 @@
         compiler_params=pltpu.CompilerParams(vmem_limit_bytes=64 * 1024 * 1024),
         cost_estimate=pl.CostEstimate(flops=1_200_000_000, bytes_accessed=4_500_000, transcendentals=700_000),
         name="item_grad",
-    )(length, *loaded)
-
-
-def sum_rows(rows_ref, bucket):
-    total = jnp.zeros((bucket.shape[0], rows_ref.shape[2]), f32)
-    for member in range(rows_ref.shape[0]):
-        ids = rows_ref[member, CAP:, :CAP].astype(f32)
+    )(length, me, *loaded)
+
+
+def sum_rows(row_refs, bucket):
+    total = jnp.zeros((bucket.shape[0], row_refs[0].shape[1]), f32)
+    for rows_ref in row_refs:
+        ids = rows_ref[CAP:, :CAP].astype(f32)
         slot_id = ids[0:1] * ID_BASE + ids[1:2]
         slot_id = jnp.where(ids[2:3] > 0.5, slot_id, -1.0).astype(jnp.int32)
         chosen = jnp.where(bucket == slot_id, 1.0, 0.0).astype(bf16)
-        total = total + dot(chosen, rows_ref[member, :CAP, :])
+        total = total + dot(chosen, rows_ref[:CAP, :])
     return total
 
 
@@ -187,7 +185,7 @@
     z = place // HOT_DEV + first
     z = jnp.where(z >= z_size, z - z_size, z)
     bucket = z * (HOT_DEV * cores) + place % HOT_DEV + base_ref[0]
-    out_ref[...] = sum_rows(rows_ref, bucket).reshape(out_ref.shape).astype(bf16)
+    out_ref[...] = sum_rows([rows_ref.at[i] for i in range(rows_ref.shape[0])], bucket).reshape(out_ref.shape).astype(bf16)
 
 
 def hot_call(z_size, cores, first, base, rows):
@@ -203,38 +201,44 @@
     )(base, rows)
 
 
-def cold_kernel(rows_ref, out_ref):
-    out_ref[...] = sum_rows(rows_ref, lax.broadcasted_iota(jnp.int32, (COLD_DEV, CAP), 0))
+def cold_kernel(*refs):
+    refs[-1][...] = sum_rows(refs[:-1], lax.broadcasted_iota(jnp.int32, (COLD_DEV, CAP), 0))
 
 
 def cold_call(rows):
     whole = pl.BlockSpec(memory_space=pltpu.VMEM)
     return pl.pallas_call(
         cold_kernel,
-        in_specs=[whole],
+        in_specs=[whole] * len(rows),
         out_specs=whole,
-        out_shape=jax.ShapeDtypeStruct((COLD_DEV, rows.shape[2]), f32),
+        out_shape=jax.ShapeDtypeStruct((COLD_DEV, rows[0].shape[1]), f32),
         compiler_params=pltpu.CompilerParams(vmem_limit_bytes=16 * 1024 * 1024),
         cost_estimate=pl.CostEstimate(flops=40_000_000, bytes_accessed=600_000, transcendentals=0),
         name="cold_sum",
-    )(rows)
+    )(*rows)
 
 
 def shards(embeddings, lengths, cotangent, w_proj, w_out, routes, hot_ids, cold_ids):
     owners = lax.axis_size("table")
     z_size, cores = lax.axis_size("z"), lax.axis_size("core")
     seq, width = embeddings.shape[1:]
-    hot_rows, cold_rows = item_call(
-        owners, lengths, embeddings.reshape(seq, width), cotangent.reshape(seq, width), w_proj, w_out,
+    me = lax.axis_index("table").reshape(1).astype(jnp.int32)
+    own_rows, *sent, hot_rows = item_call(
+        owners, lengths, me, embeddings.reshape(seq, width), cotangent.reshape(seq, width), w_proj, w_out,
         routes.reshape(1, seq), hot_ids, cold_ids,
     )
-    cold_grad = cold_call(lax.all_to_all(cold_rows, "table", 0, 0))
     gathered = lax.all_gather(hot_rows, ("y", "core"))
     base = lax.axis_index("y") * (z_size * cores * HOT_DEV) + lax.axis_index("core") * HOT_DEV
     first = z_size * 5 // 8
     order = [(first + i) % z_size for i in range(z_size)]
     partial = hot_call(z_size, cores, first, base.reshape(1).astype(jnp.int32), gathered)
+    partial, sent = lax.optimization_barrier((partial, sent))
     parts = lax.all_to_all(partial, "z", 0, 0, axis_index_groups=[order])
+    received = [
+        lax.ppermute(rows, "table", [(i, (i + step) % owners) for i in range(owners)])
+        for step, rows in enumerate(sent, start=1)
+    ]
+    cold_grad = cold_call([*received, own_rows])
     share = jnp.sum(parts.astype(f32), axis=0)
     hot_grad = lax.psum(share, "table")
     return (hot_grad, cold_grad)

time: 87.3 us -> 82.5 us (0.945)
  waiting for transfers between devices: 15.8 us -> 3.48 us
  starting transfers between devices: 26 us -> 32.3 us
  local copies, waits for them, and re-layouts: 0 us -> 0.89 us
    all_to_all x1, waiting for transfers between devices: 15.8 us -> 0.28 us  [shards(): parts = lax.all_to_all(partial, 'z', 0, 0, axis_index_groups=[order])]
    ppermute x0 -> x3, starting transfers between devices: none -> 11.4 us  [shards(): lax.ppermute(rows, 'table', [(i, (i + step) % owners) for i in range(owne...]
    all_to_all x1 -> x0, starting transfers between devices: 4.29 us -> none  [shards(): cold_grad = cold_call(lax.all_to_all(cold_rows, 'table', 0, 0))]
    ppermute x0 -> x3, waiting for transfers between devices: none -> 3.2 us  [shards(): lax.ppermute(rows, 'table', [(i, (i + step) % owners) for i in range(owne...]
    unnamed x0 -> x2, local copies, waits for them, and re-layouts: none -> 0.89 us
  transfers between devices with their start and end apart: 2 -> 4, of which waited for: 1 -> 3; matrix products, arithmetic and copies ran while one was open for 0% -> 0% of each run, Pallas kernels for 2% -> 1%
where the time goes in v3:
time: 82.5 us; the launch traced here: 81.9 us
  blocking collectives  34.8 us (42%)
  starting transfers between devices  32.3 us (39%)
  Pallas kernels  9.07 us (11%)
  waiting for transfers between devices  3.48 us (4%)
  between operations  1.34 us (2%)
  local copies, waits for them, and re-layouts  0.89 us (1%)
    all_gather x1, blocking collectives, shards(): gathered = lax.all_gather(hot_rows, ('y', 'core'))  23.6 us
    all_to_all x1, starting transfers between devices, shards(): parts = lax.all_to_all(partial, 'z', 0, 0, axis_index_groups=[order])  20.9 us
    ppermute x3, starting transfers between devices, shards(): lax.ppermute(rows, 'table', [(i, (i + step) % owners) for i in range(owne...  11.4 us
    psum x1, blocking collectives, shards(): hot_grad = lax.psum(share, 'table')  11.2 us
    pallas_call x1, Pallas kernels, item_call(): pl.pallas_call(functools.partial(item_kernel, owners), in_specs=[pl.Block...  7.02 us
    ppermute x3, waiting for transfers between devices, shards(): lax.ppermute(rows, 'table', [(i, (i + step) % owners) for i in range(owne...  3.2 us
  transfers between devices with their start and end apart: 4, of which 3 were waited for; matrix products, arithmetic and copies ran while one was open for 0% of the time, Pallas kernels for 1%

profile of v3, /device:TPU:24, one launch (start us, length us, event | category | flops | bytes accessed | tf_op | source)
XLA Modules:
  0.0 81.9 jit_solution(2434112693752663590)
XLA Ops:
  1.3 7.0 %item_grad.1 = (bf16[80,512]{1,0:T(8,128)(2,1)}, bf16[80,512]{1,0:T(8,128)(2,1)}, bf16[80,512]{1,0:T(8,128)(2,1)}, bf16[80,512]{1,0:T(8,128)(2,1)}, bf16[80,512]{1,0:T(8,128)(2,1)}) custom-call(s32[1]{0:T(128)S(6)} %copy.10.refs_0_, s32[1]{0:T(128)} %bitcast.1.refs_1_, bf16[192,512]{1,0:T(8,128)(2,1)} %bitcast.7, bf16[192,512]{1,0:T(8,128)(2,1)} %bitcast.8, ...), custom_call_target="tpu_custom_call" | custom-call | flops 1200000000 | bytes 4500000 | tf_op jit(solution)/shard_map/item_grad/pallas_call | solution.py:150
  8.3 23.6 %all-gather = bf16[640,512]{1,0:T(8,128)(2,1)S(1)} all-gather(bf16[80,512]{1,0:T(8,128)(2,1)} %get-tuple-element.11), channel_id=2, replica_groups=mesh['y'=4,'z'=32,'core'=2,'table'=4] {'y','core'}, dimensions={0}, use_global_device_ids=true | all-gather | bytes 737280 | tf_op jit(solution)/shard_map/all_gather | solution.py:230
  31.9 1.1 %hot_sum.1 = bf16[32,4,512]{2,1,0:T(4,128)(2,1)} custom-call(s32[1]{0:T(128)} %bitcast.base_ref, bf16[8,80,512]{2,1,0:T(8,128)(2,1)S(1)} %bitcast.6), custom_call_target="tpu_custom_call" | custom-call | flops 80000000 | bytes 800000 | tf_op jit(solution)/shard_map/hot_sum/pallas_call | solution.py:193
  33.0 20.9 %all-to-all-start = ((bf16[32,4,512]{2,1,0:T(4,128)(2,1)}), bf16[32,4,512]{2,1,0:T(4,128)(2,1)S(1)}, u32[]{:S(2)}, u32[]{:S(2)}) async-start(bf16[32,4,512]{2,1,0:T(4,128)(2,1)} %hot_sum.1), calls=%async_computation | async-start | bytes 262144 | tf_op jit(solution)/shard_map/all_to_all | solution.py:236
  53.9 3.4 %collective-permute-start = (bf16[80,512]{1,0:T(8,128)(2,1)}, bf16[80,512]{1,0:T(8,128)(2,1)S(1)}, u32[]{:S(2)}, u32[]{:S(2)}) collective-permute-start(bf16[80,512]{1,0:T(8,128)(2,1)} %get-tuple-element.16), channel_id=1, source_target_pairs={{0,1},{1,2},{2,3},{3,0},{4,5},{5,6},{6,7},{7,4},{8,9},{9,10},{10,1... | collective-permute-start | bytes 245768 | tf_op jit(solution)/shard_map/ppermute | solution.py:238
  57.4 4.6 %collective-permute-start.1 = (bf16[80,512]{1,0:T(8,128)(2,1)}, bf16[80,512]{1,0:T(8,128)(2,1)S(1)}, u32[]{:S(2)}, u32[]{:S(2)}) collective-permute-start(bf16[80,512]{1,0:T(8,128)(2,1)} %get-tuple-element.17), channel_id=1, source_target_pairs={{0,2},{1,3},{2,0},{3,1},{4,6},{5,7},{6,4},{7,5},{8,10},{9,11},{10,... | collective-permute-start | bytes 245768 | tf_op jit(solution)/shard_map/ppermute | solution.py:238
  62.0 3.3 %collective-permute-start.2 = (bf16[80,512]{1,0:T(8,128)(2,1)}, bf16[80,512]{1,0:T(8,128)(2,1)S(1)}, u32[]{:S(2)}, u32[]{:S(2)}) collective-permute-start(bf16[80,512]{1,0:T(8,128)(2,1)} %get-tuple-element.18), channel_id=1, source_target_pairs={{0,3},{1,0},{2,1},{3,2},{4,7},{5,4},{6,5},{7,6},{8,11},{9,8},{10,9... | collective-permute-start | bytes 245768 | tf_op jit(solution)/shard_map/ppermute | solution.py:238
  65.3 0.0 collective-permute-done.refs_0_
  65.3 0.1 collective-permute-done.1.refs_1_
  65.4 3.1 %collective-permute-done.2.refs_2_ = bf16[80,512]{1,0:T(8,128)(2,1)S(1)} collective-permute-done((bf16[80,512]{1,0:T(8,128)(2,1)}, bf16[80,512]{1,0:T(8,128)(2,1)S(1)}, u32[]{:S(2)}, u32[]{:S(2)}) %collective-permute-start.2) | collective-permute-done | bytes 81952 | tf_op jit(solution)/shard_map/ppermute | solution.py:238
  68.5 0.0 copy-start
  68.5 0.9 %copy-done = bf16[80,512]{1,0:T(8,128)(2,1)S(1)} copy-done((bf16[80,512]{1,0:T(8,128)(2,1)S(1)}, bf16[80,512]{1,0:T(8,128)(2,1)}, u32[]{:S(2)}) %copy-start) | copy-done | bytes 81944
  69.4 1.0 %cold_sum.1 = f32[128,512]{1,0:T(8,128)} custom-call(bf16[80,512]{1,0:T(8,128)(2,1)S(1)} %collective-permute-done.refs_0_, bf16[80,512]{1,0:T(8,128)(2,1)S(1)} %collective-permute-done.1.refs_1_, bf16[80,512]{1,0:T(8,128)(2,1)S(1)} %collective-permute-done.2.refs_2_, bf16[80,512]{1,0:T(8,128)(2,1)S(1)} %copy-done), custom_call_target="tpu_custom_call" | custom-call | flops 40000000 | bytes 600000 | tf_op jit(solution)/shard_map/cold_sum/pallas_call | solution.py:210
  70.4 0.3 all-to-all-done
  70.7 0.1 convert_reduce_fusion
  70.8 11.2 %psum.7 = f32[4,512]{1,0:T(4,128)} all-reduce(f32[4,512]{1,0:T(4,128)S(1)} %convert_reduce_fusion), channel_id=1, replica_groups=mesh['y'=4,'z'=32,'core'=2,'table'=4] {'table'}, use_global_device_ids=true, to_apply=%region_1.0 | all-reduce | flops 2048 | bytes 16384 | tf_op jit(solution)/shard_map/psum | solution.py:243
Async XLA Ops:
  33.0 37.7 %all-to-all-start = ((bf16[32,4,512]{2,1,0:T(4,128)(2,1)}), bf16[32,4,512]{2,1,0:T(4,128)(2,1)S(1)}, u32[]{:S(2)}, u32[]{:S(2)}) async-start(bf16[32,4,512]{2,1,0:T(4,128)(2,1)} %hot_sum.1), calls=%async_computation | async-start | bytes 262144 | tf_op jit(solution)/shard_map/all_to_all | solution.py:236
  53.9 11.4 %collective-permute-start = (bf16[80,512]{1,0:T(8,128)(2,1)}, bf16[80,512]{1,0:T(8,128)(2,1)S(1)}, u32[]{:S(2)}, u32[]{:S(2)}) collective-permute-start(bf16[80,512]{1,0:T(8,128)(2,1)} %get-tuple-element.16), channel_id=1, source_target_pairs={{0,1},{1,2},{2,3},{3,0},{4,5},{5,6},{6,7},{7,4},{8,9},{9,10},{10,1... | collective-permute-start | bytes 245768 | tf_op jit(solution)/shard_map/ppermute | solution.py:238
  57.4 8.0 %collective-permute-start.1 = (bf16[80,512]{1,0:T(8,128)(2,1)}, bf16[80,512]{1,0:T(8,128)(2,1)S(1)}, u32[]{:S(2)}, u32[]{:S(2)}) collective-permute-start(bf16[80,512]{1,0:T(8,128)(2,1)} %get-tuple-element.17), channel_id=1, source_target_pairs={{0,2},{1,3},{2,0},{3,1},{4,6},{5,7},{6,4},{7,5},{8,10},{9,11},{10,... | collective-permute-start | bytes 245768 | tf_op jit(solution)/shard_map/ppermute | solution.py:238
  62.0 6.5 %collective-permute-start.2 = (bf16[80,512]{1,0:T(8,128)(2,1)}, bf16[80,512]{1,0:T(8,128)(2,1)S(1)}, u32[]{:S(2)}, u32[]{:S(2)}) collective-permute-start(bf16[80,512]{1,0:T(8,128)(2,1)} %get-tuple-element.18), channel_id=1, source_target_pairs={{0,3},{1,0},{2,1},{3,2},{4,7},{5,4},{6,5},{7,6},{8,11},{9,8},{10,9... | collective-permute-start | bytes 245768 | tf_op jit(solution)/shard_map/ppermute | solution.py:238
  68.5 0.9 %copy-start = (bf16[80,512]{1,0:T(8,128)(2,1)S(1)}, bf16[80,512]{1,0:T(8,128)(2,1)}, u32[]{:S(2)}) copy-start(bf16[80,512]{1,0:T(8,128)(2,1)} %get-tuple-element.19.refs_3_) | copy-start | bytes 245764

commit v4 on v3

--- a/solution.py
+++ b/solution.py
@@ -182,8 +182,8 @@
 def hot_kernel(cores, first, base_ref, rows_ref, out_ref):
     z_size = out_ref.shape[0]
     place = lax.broadcasted_iota(jnp.int32, (z_size * HOT_DEV, CAP), 0)
-    z = place // HOT_DEV + first
-    z = jnp.where(z >= z_size, z - z_size, z)
+    z = first - place // HOT_DEV
+    z = jnp.where(z < 0, z + z_size, z)
     bucket = z * (HOT_DEV * cores) + place % HOT_DEV + base_ref[0]
     out_ref[...] = sum_rows([rows_ref.at[i] for i in range(rows_ref.shape[0])], bucket).reshape(out_ref.shape).astype(bf16)
 
@@ -216,6 +216,27 @@
         cost_estimate=pl.CostEstimate(flops=40_000_000, bytes_accessed=600_000, transcendentals=0),
         name="cold_sum",
     )(*rows)
+
+
+def spread_kernel(parts_ref, out_ref):
+    total = parts_ref[0].astype(f32)
+    for i in range(1, parts_ref.shape[0]):
+        total = total + parts_ref[i].astype(f32)
+    for i in range(out_ref.shape[0]):
+        out_ref[i] = total
+
+
+def spread_call(owners, parts):
+    whole = pl.BlockSpec(memory_space=pltpu.VMEM)
+    return pl.pallas_call(
+        spread_kernel,
+        in_specs=[whole],
+        out_specs=whole,
+        out_shape=jax.ShapeDtypeStruct((owners,) + parts.shape[1:], f32),
+        compiler_params=pltpu.CompilerParams(vmem_limit_bytes=16 * 1024 * 1024),
+        cost_estimate=pl.CostEstimate(flops=70_000, bytes_accessed=160_000, transcendentals=0),
+        name="spread",
+    )(parts)
 
 
 def shards(embeddings, lengths, cotangent, w_proj, w_out, routes, hot_ids, cold_ids):
@@ -230,7 +251,7 @@
     gathered = lax.all_gather(hot_rows, ("y", "core"))
     base = lax.axis_index("y") * (z_size * cores * HOT_DEV) + lax.axis_index("core") * HOT_DEV
     first = z_size * 5 // 8
-    order = [(first + i) % z_size for i in range(z_size)]
+    order = [(first - i) % z_size for i in range(z_size)]
     partial = hot_call(z_size, cores, first, base.reshape(1).astype(jnp.int32), gathered)
     partial, sent = lax.optimization_barrier((partial, sent))
     parts = lax.all_to_all(partial, "z", 0, 0, axis_index_groups=[order])
@@ -239,8 +260,9 @@
         for step, rows in enumerate(sent, start=1)
     ]
     cold_grad = cold_call([*received, own_rows])
-    share = jnp.sum(parts.astype(f32), axis=0)
-    hot_grad = lax.psum(share, "table")
+    last = [(owners - 1 + i) % owners for i in range(owners)]
+    copies = lax.all_to_all(spread_call(owners, parts), "table", 0, 0, axis_index_groups=[last])
+    hot_grad = jnp.sum(copies, axis=0)
     return (hot_grad, cold_grad)
 
 

time: 82.5 us -> 81.9 us (level)
  blocking collectives: 34.8 us -> 23.6 us
  starting transfers between devices: 32.3 us -> 38.3 us
  waiting for transfers between devices: 3.48 us -> 6.7 us
    psum x1 -> x0, blocking collectives: 11.2 us -> none  [shards(): hot_grad = lax.psum(share, 'table')]
    all_to_all x0 -> x1, starting transfers between devices: none -> 6 us  [shards(): lax.all_to_all(spread_call(owners, parts), 'table', 0, 0, axis_index_grou...]
    all_to_all x1, waiting for transfers between devices: 0.28 us -> 5.19 us  [shards(): parts = lax.all_to_all(partial, 'z', 0, 0, axis_index_groups=[order])]
    ppermute x3, waiting for transfers between devices: 3.2 us -> 0.01 us  [shards(): lax.ppermute(rows, 'table', [(i, (i + step) % owners) for i in range(owne...]
    all_to_all x0 -> x1, waiting for transfers between devices: none -> 1.5 us  [shards(): lax.all_to_all(spread_call(owners, parts), 'table', 0, 0, axis_index_grou...]
  transfers between devices with their start and end apart: 4 -> 5, of which waited for: 3 -> 2; matrix products, arithmetic and copies ran while one was open for 0% -> 0% of each run, Pallas kernels for 1% -> 2%
where the time goes in v4:
time: 81.9 us; the launch traced here: 81.2 us
  starting transfers between devices  38.3 us (47%)
  blocking collectives  23.6 us (29%)
  Pallas kernels  9.75 us (12%)
  waiting for transfers between devices  6.7 us (8%)
  between operations  1.34 us (2%)
  local copies, waits for them, and re-layouts  0.88 us (1%)
    all_gather x1, blocking collectives, shards(): gathered = lax.all_gather(hot_rows, ('y', 'core'))  23.6 us
    all_to_all x1, starting transfers between devices, shards(): parts = lax.all_to_all(partial, 'z', 0, 0, axis_index_groups=[order])  20.9 us
    ppermute x3, starting transfers between devices, shards(): lax.ppermute(rows, 'table', [(i, (i + step) % owners) for i in range(owne...  11.4 us
    pallas_call x1, Pallas kernels, item_call(): pl.pallas_call(functools.partial(item_kernel, owners), in_specs=[pl.Block...  7.04 us
    all_to_all x1, starting transfers between devices, shards(): lax.all_to_all(spread_call(owners, parts), 'table', 0, 0, axis_index_grou...  6 us
    all_to_all x1, waiting for transfers between devices, shards(): parts = lax.all_to_all(partial, 'z', 0, 0, axis_index_groups=[order])  5.19 us
  transfers between devices with their start and end apart: 5, of which 2 were waited for; matrix products, arithmetic and copies ran while one was open for 0% of the time, Pallas kernels for 2%

profile of v4, /device:TPU:24, one launch (start us, length us, event | category | flops | bytes accessed | tf_op | source)
XLA Modules:
  0.0 81.2 jit_solution(9912320875523617809)
XLA Ops:
  1.3 7.0 %item_grad.1 = (bf16[80,512]{1,0:T(8,128)(2,1)}, bf16[80,512]{1,0:T(8,128)(2,1)}, bf16[80,512]{1,0:T(8,128)(2,1)}, bf16[80,512]{1,0:T(8,128)(2,1)}, bf16[80,512]{1,0:T(8,128)(2,1)}) custom-call(s32[1]{0:T(128)S(6)} %copy.10.refs_0_, s32[1]{0:T(128)} %bitcast.1.refs_1_, bf16[192,512]{1,0:T(8,128)(2,1)} %bitcast.7, bf16[192,512]{1,0:T(8,128)(2,1)} %bitcast.8, ...), custom_call_target="tpu_custom_call" | custom-call | flops 1200000000 | bytes 4500000 | tf_op jit(solution)/shard_map/item_grad/pallas_call | solution.py:150
  8.3 23.6 %all-gather = bf16[640,512]{1,0:T(8,128)(2,1)S(1)} all-gather(bf16[80,512]{1,0:T(8,128)(2,1)} %get-tuple-element.11), channel_id=2, replica_groups=mesh['y'=4,'z'=32,'core'=2,'table'=4] {'y','core'}, dimensions={0}, use_global_device_ids=true | all-gather | bytes 737280 | tf_op jit(solution)/shard_map/all_gather | solution.py:251
  32.0 1.1 %hot_sum.1 = bf16[32,4,512]{2,1,0:T(4,128)(2,1)} custom-call(s32[1]{0:T(128)} %bitcast.base_ref, bf16[8,80,512]{2,1,0:T(8,128)(2,1)S(1)} %bitcast.6), custom_call_target="tpu_custom_call" | custom-call | flops 80000000 | bytes 800000 | tf_op jit(solution)/shard_map/hot_sum/pallas_call | solution.py:193
  33.0 20.9 %all-to-all-start = ((bf16[32,4,512]{2,1,0:T(4,128)(2,1)}), bf16[32,4,512]{2,1,0:T(4,128)(2,1)S(1)}, u32[]{:S(2)}, u32[]{:S(2)}) async-start(bf16[32,4,512]{2,1,0:T(4,128)(2,1)} %hot_sum.1), calls=%async_computation | async-start | bytes 262144 | tf_op jit(solution)/shard_map/all_to_all | solution.py:257
  54.0 3.4 %collective-permute-start = (bf16[80,512]{1,0:T(8,128)(2,1)}, bf16[80,512]{1,0:T(8,128)(2,1)S(1)}, u32[]{:S(2)}, u32[]{:S(2)}) collective-permute-start(bf16[80,512]{1,0:T(8,128)(2,1)} %get-tuple-element.16), channel_id=1, source_target_pairs={{0,1},{1,2},{2,3},{3,0},{4,5},{5,6},{6,7},{7,4},{8,9},{9,10},{10,1... | collective-permute-start | bytes 245768 | tf_op jit(solution)/shard_map/ppermute | solution.py:259
  57.4 4.6 %collective-permute-start.1 = (bf16[80,512]{1,0:T(8,128)(2,1)}, bf16[80,512]{1,0:T(8,128)(2,1)S(1)}, u32[]{:S(2)}, u32[]{:S(2)}) collective-permute-start(bf16[80,512]{1,0:T(8,128)(2,1)} %get-tuple-element.17), channel_id=1, source_target_pairs={{0,2},{1,3},{2,0},{3,1},{4,6},{5,7},{6,4},{7,5},{8,10},{9,11},{10,... | collective-permute-start | bytes 245768 | tf_op jit(solution)/shard_map/ppermute | solution.py:259
  62.0 3.3 %collective-permute-start.2 = (bf16[80,512]{1,0:T(8,128)(2,1)}, bf16[80,512]{1,0:T(8,128)(2,1)S(1)}, u32[]{:S(2)}, u32[]{:S(2)}) collective-permute-start(bf16[80,512]{1,0:T(8,128)(2,1)} %get-tuple-element.18), channel_id=1, source_target_pairs={{0,3},{1,0},{2,1},{3,2},{4,7},{5,4},{6,5},{7,6},{8,11},{9,8},{10,9... | collective-permute-start | bytes 245768 | tf_op jit(solution)/shard_map/ppermute | solution.py:259
  65.4 5.2 %all-to-all-done.parts_ref = bf16[32,4,512]{2,1,0:T(4,128)(2,1)S(1)} async-done(((bf16[32,4,512]{2,1,0:T(4,128)(2,1)}), bf16[32,4,512]{2,1,0:T(4,128)(2,1)S(1)}, u32[]{:S(2)}, u32[]{:S(2)}) %all-to-all-start) | async-done | bytes 131104 | tf_op jit(solution)/shard_map/all_to_all | solution.py:257
  70.6 0.6 spread.1
  71.2 6.0 %all-to-all-start.1 = ((f32[4,4,512]{2,1,0:T(4,128)}), f32[4,4,512]{2,1,0:T(4,128)S(1)}, u32[]{:S(2)}, u32[]{:S(2)}) async-start(f32[4,4,512]{2,1,0:T(4,128)} %spread.1), calls=%async_computation.1 | async-start | bytes 65536 | tf_op jit(solution)/shard_map/all_to_all | solution.py:264
  77.2 0.0 collective-permute-done.refs_0_
  77.2 0.0 collective-permute-done.1.refs_1_
  77.2 0.0 collective-permute-done.2.refs_2_
  77.2 0.0 copy-start
  77.2 0.9 %copy-done = bf16[80,512]{1,0:T(8,128)(2,1)S(1)} copy-done((bf16[80,512]{1,0:T(8,128)(2,1)S(1)}, bf16[80,512]{1,0:T(8,128)(2,1)}, u32[]{:S(2)}) %copy-start) | copy-done | bytes 81944
  78.1 1.0 %cold_sum.1 = f32[128,512]{1,0:T(8,128)} custom-call(bf16[80,512]{1,0:T(8,128)(2,1)S(1)} %collective-permute-done.refs_0_, bf16[80,512]{1,0:T(8,128)(2,1)S(1)} %collective-permute-done.1.refs_1_, bf16[80,512]{1,0:T(8,128)(2,1)S(1)} %collective-permute-done.2.refs_2_, bf16[80,512]{1,0:T(8,128)(2,1)S(1)} %copy-done), custom_call_target="tpu_custom_call" | custom-call | flops 40000000 | bytes 600000 | tf_op jit(solution)/shard_map/cold_sum/pallas_call | solution.py:210
  79.1 1.5 %all-to-all-done.1 = f32[4,4,512]{2,1,0:T(4,128)S(1)} async-done(((f32[4,4,512]{2,1,0:T(4,128)}), f32[4,4,512]{2,1,0:T(4,128)S(1)}, u32[]{:S(2)}, u32[]{:S(2)}) %all-to-all-start.1) | async-done | bytes 32800 | tf_op jit(solution)/shard_map/all_to_all | solution.py:264
  80.6 0.6 reduce_sum.9
Async XLA Ops:
  33.0 37.5 %all-to-all-start = ((bf16[32,4,512]{2,1,0:T(4,128)(2,1)}), bf16[32,4,512]{2,1,0:T(4,128)(2,1)S(1)}, u32[]{:S(2)}, u32[]{:S(2)}) async-start(bf16[32,4,512]{2,1,0:T(4,128)(2,1)} %hot_sum.1), calls=%async_computation | async-start | bytes 262144 | tf_op jit(solution)/shard_map/all_to_all | solution.py:257
  54.0 23.2 %collective-permute-start = (bf16[80,512]{1,0:T(8,128)(2,1)}, bf16[80,512]{1,0:T(8,128)(2,1)S(1)}, u32[]{:S(2)}, u32[]{:S(2)}) collective-permute-start(bf16[80,512]{1,0:T(8,128)(2,1)} %get-tuple-element.16), channel_id=1, source_target_pairs={{0,1},{1,2},{2,3},{3,0},{4,5},{5,6},{6,7},{7,4},{8,9},{9,10},{10,1... | collective-permute-start | bytes 245768 | tf_op jit(solution)/shard_map/ppermute | solution.py:259
  57.4 19.8 %collective-permute-start.1 = (bf16[80,512]{1,0:T(8,128)(2,1)}, bf16[80,512]{1,0:T(8,128)(2,1)S(1)}, u32[]{:S(2)}, u32[]{:S(2)}) collective-permute-start(bf16[80,512]{1,0:T(8,128)(2,1)} %get-tuple-element.17), channel_id=1, source_target_pairs={{0,2},{1,3},{2,0},{3,1},{4,6},{5,7},{6,4},{7,5},{8,10},{9,11},{10,... | collective-permute-start | bytes 245768 | tf_op jit(solution)/shard_map/ppermute | solution.py:259
  62.0 15.2 %collective-permute-start.2 = (bf16[80,512]{1,0:T(8,128)(2,1)}, bf16[80,512]{1,0:T(8,128)(2,1)S(1)}, u32[]{:S(2)}, u32[]{:S(2)}) collective-permute-start(bf16[80,512]{1,0:T(8,128)(2,1)} %get-tuple-element.18), channel_id=1, source_target_pairs={{0,3},{1,0},{2,1},{3,2},{4,7},{5,4},{6,5},{7,6},{8,11},{9,8},{10,9... | collective-permute-start | bytes 245768 | tf_op jit(solution)/shard_map/ppermute | solution.py:259
  71.2 9.4 %all-to-all-start.1 = ((f32[4,4,512]{2,1,0:T(4,128)}), f32[4,4,512]{2,1,0:T(4,128)S(1)}, u32[]{:S(2)}, u32[]{:S(2)}) async-start(f32[4,4,512]{2,1,0:T(4,128)} %spread.1), calls=%async_computation.1 | async-start | bytes 65536 | tf_op jit(solution)/shard_map/all_to_all | solution.py:264
  77.2 0.9 %copy-start = (bf16[80,512]{1,0:T(8,128)(2,1)S(1)}, bf16[80,512]{1,0:T(8,128)(2,1)}, u32[]{:S(2)}) copy-start(bf16[80,512]{1,0:T(8,128)(2,1)} %get-tuple-element.19.refs_3_) | copy-start | bytes 245764

commit v5 on v4

--- a/solution.py
+++ b/solution.py
@@ -136,13 +136,22 @@
     slots = lax.broadcasted_iota(jnp.int32, (CAP, seq), 0)
     for step, out in enumerate(outs):
         chosen = jnp.where(slots == place[step : step + 1], 1.0, 0.0).astype(bf16)
-        out[:CAP, :] = dot(chosen, grad_rows).astype(bf16)
+        sent = dot(chosen, grad_rows).astype(bf16)
         slot_ids = dot(ids, chosen, ((1,), (1,)))
-        out[CAP:, :] = jnp.zeros((ID_ROWS, width), bf16)
-        out[CAP:, :PAIR] = jnp.concatenate([slot_ids, jnp.zeros((ID_ROWS, PAIR - CAP), f32)], axis=1).astype(bf16)
-
-
-def item_call(owners, length, me, emb, cot, w_proj, w_out, routes, hot_ids, cold_ids):
+        slot_ids = jnp.concatenate([slot_ids, jnp.zeros((ID_ROWS, PAIR - CAP), f32)], axis=1).astype(bf16)
+        if step < owners:
+            out[:CAP, :] = sent
+            out[CAP:, :] = jnp.zeros((ID_ROWS, width), bf16)
+            out[CAP:, :PAIR] = slot_ids
+        else:
+            piece = width // owners
+            for block in range(out.shape[0]):
+                start = block % owners * piece
+                out[block, :CAP, :] = sent[:, start : start + piece]
+                out[block, CAP:, :] = slot_ids
+
+
+def item_call(owners, near, length, me, emb, cot, w_proj, w_out, routes, hot_ids, cold_ids):
     seq, width = emb.shape
     pairs = width // PAIR
     whole = pl.BlockSpec(memory_space=pltpu.VMEM)
@@ -151,7 +160,8 @@
         functools.partial(item_kernel, owners),
         in_specs=[pl.BlockSpec(memory_space=pltpu.SMEM)] * 2 + [pl.BlockSpec(memory_space=pltpu.HBM)] * 7,
         out_specs=[whole] * (owners + 1),
-        out_shape=[jax.ShapeDtypeStruct((CAP + ID_ROWS, width), bf16)] * (owners + 1),
+        out_shape=[jax.ShapeDtypeStruct((CAP + ID_ROWS, width), bf16)] * owners
+        + [jax.ShapeDtypeStruct((near * owners, CAP + ID_ROWS, width // owners), bf16)],
         scratch_shapes=[pltpu.VMEM(a.shape, a.dtype) for a in loaded]
         + [
             pltpu.VMEM((seq, 4 * width), bf16),
@@ -245,10 +255,10 @@
     seq, width = embeddings.shape[1:]
     me = lax.axis_index("table").reshape(1).astype(jnp.int32)
     own_rows, *sent, hot_rows = item_call(
-        owners, lengths, me, embeddings.reshape(seq, width), cotangent.reshape(seq, width), w_proj, w_out,
+        owners, lax.axis_size("y") * cores, lengths, me, embeddings.reshape(seq, width), cotangent.reshape(seq, width), w_proj, w_out,
         routes.reshape(1, seq), hot_ids, cold_ids,
     )
-    gathered = lax.all_gather(hot_rows, ("y", "core"))
+    gathered = lax.all_to_all(hot_rows, ("y", "core", "table"), 0, 0)
     base = lax.axis_index("y") * (z_size * cores * HOT_DEV) + lax.axis_index("core") * HOT_DEV
     first = z_size * 5 // 8
     order = [(first - i) % z_size for i in range(z_size)]
@@ -260,9 +270,8 @@
         for step, rows in enumerate(sent, start=1)
     ]
     cold_grad = cold_call([*received, own_rows])
-    last = [(owners - 1 + i) % owners for i in range(owners)]
-    copies = lax.all_to_all(spread_call(owners, parts), "table", 0, 0, axis_index_groups=[last])
-    hot_grad = jnp.sum(copies, axis=0)
+    copies = lax.all_to_all(spread_call(owners, parts), "table", 0, 0)
+    hot_grad = jnp.transpose(copies, (1, 0, 2)).reshape(HOT_DEV, width)
     return (hot_grad, cold_grad)
 
 

time: 81.9 us -> 81 us (0.989)
  the two profiles are of different devices: /device:TPU:24 before, /device:TPU:32 now
where the time goes in v5:
time: 81 us; the launch traced here: 80.6 us
  starting transfers between devices  51.2 us (63%)
  waiting for transfers between devices  17.4 us (21%)
  Pallas kernels  9.92 us (12%)
  between operations  1.37 us (2%)
    all_to_all x1, starting transfers between devices, shards(): parts = lax.all_to_all(partial, 'z', 0, 0, axis_index_groups=[order])  30.6 us
    all_to_all x1, waiting for transfers between devices, shards(): gathered = lax.all_to_all(hot_rows, ('y', 'core', 'table'), 0, 0)  13.1 us
    ppermute x3, starting transfers between devices, shards(): lax.ppermute(rows, 'table', [(i, (i + step) % owners) for i in range(owne...  9.58 us
    all_to_all x1, starting transfers between devices, shards(): gathered = lax.all_to_all(hot_rows, ('y', 'core', 'table'), 0, 0)  7.47 us
    pallas_call x1, Pallas kernels, item_call(): pl.pallas_call(functools.partial(item_kernel, owners), in_specs=[pl.Block...  7.27 us
    all_to_all x1, waiting for transfers between devices, shards(): copies = lax.all_to_all(spread_call(owners, parts), 'table', 0, 0)  4.3 us
    all_to_all x1, starting transfers between devices, shards(): copies = lax.all_to_all(spread_call(owners, parts), 'table', 0, 0)  3.57 us
  transfers between devices with their start and end apart: 6, of which 2 were waited for; matrix products, arithmetic and copies ran while one was open for 0% of the time, Pallas kernels for 2%

profile of v5, /device:TPU:32, one launch (start us, length us, event | category | flops | bytes accessed | tf_op | source)
XLA Modules:
  0.0 80.6 jit_solution(8660468172281315755)
XLA Ops:
  1.3 7.3 %item_grad.1 = (bf16[80,512]{1,0:T(8,128)(2,1)}, bf16[80,512]{1,0:T(8,128)(2,1)}, bf16[80,512]{1,0:T(8,128)(2,1)}, bf16[80,512]{1,0:T(8,128)(2,1)}, bf16[32,80,128]{2,1,0:T(8,128)(2,1)}) custom-call(s32[1]{0:T(128)S(6)} %copy.11.refs_0_, s32[1]{0:T(128)} %bitcast.1.refs_1_, bf16[192,512]{1,0:T(8,128)(2,1)} %bitcast.9, bf16[192,512]{1,0:T(8,128)(2,1)} %bitcast.10, ...), custom_call_target="tpu_custom_call" | custom-call | flops 1200000000 | bytes 4500000 | tf_op jit(solution)/shard_map/item_grad/pallas_call | solution.py:159
  8.6 0.0 copy-start
  8.6 7.5 %all-to-all-start = ((bf16[32,80,128]{2,1,0:T(8,128)(2,1)}), bf16[32,80,128]{2,1,0:T(8,128)(2,1)S(1)}, u32[]{:S(2)}, u32[]{:S(2)}) async-start(bf16[32,80,128]{2,1,0:T(8,128)(2,1)} %get-tuple-element.11), calls=%async_computation | async-start | bytes 1310720 | tf_op jit(solution)/shard_map/all_to_all | solution.py:261
  16.1 13.1 %all-to-all-done.rows_ref = bf16[32,80,128]{2,1,0:T(8,128)(2,1)S(1)} async-done(((bf16[32,80,128]{2,1,0:T(8,128)(2,1)}), bf16[32,80,128]{2,1,0:T(8,128)(2,1)S(1)}, u32[]{:S(2)}, u32[]{:S(2)}) %all-to-all-start) | async-done | bytes 655392 | tf_op jit(solution)/shard_map/all_to_all | solution.py:261
  29.1 1.0 %hot_sum.1 = bf16[32,4,128]{2,1,0:T(4,128)(2,1)} custom-call(s32[1]{0:T(128)} %bitcast.base_ref, bf16[32,80,128]{2,1,0:T(8,128)(2,1)S(1)} %all-to-all-done.rows_ref), custom_call_target="tpu_custom_call" | custom-call | flops 80000000 | bytes 800000 | tf_op jit(solution)/shard_map/hot_sum/pallas_call | solution.py:203
  30.2 30.6 %all-to-all-start.1 = ((bf16[32,4,128]{2,1,0:T(4,128)(2,1)}), bf16[32,4,128]{2,1,0:T(4,128)(2,1)S(1)}, u32[]{:S(2)}, u32[]{:S(2)}) async-start(bf16[32,4,128]{2,1,0:T(4,128)(2,1)} %hot_sum.1), calls=%async_computation.1 | async-start | bytes 65536 | tf_op jit(solution)/shard_map/all_to_all | solution.py:267
  60.8 1.9 %collective-permute-start = (bf16[80,512]{1,0:T(8,128)(2,1)}, bf16[80,512]{1,0:T(8,128)(2,1)S(1)}, u32[]{:S(2)}, u32[]{:S(2)}) collective-permute-start(bf16[80,512]{1,0:T(8,128)(2,1)} %get-tuple-element.16), channel_id=1, source_target_pairs={{0,1},{1,2},{2,3},{3,0},{4,5},{5,6},{6,7},{7,4},{8,9},{9,10},{10,1... | collective-permute-start | bytes 245768 | tf_op jit(solution)/shard_map/ppermute | solution.py:269
  62.7 4.4 %collective-permute-start.1 = (bf16[80,512]{1,0:T(8,128)(2,1)}, bf16[80,512]{1,0:T(8,128)(2,1)S(1)}, u32[]{:S(2)}, u32[]{:S(2)}) collective-permute-start(bf16[80,512]{1,0:T(8,128)(2,1)} %get-tuple-element.17), channel_id=1, source_target_pairs={{0,2},{1,3},{2,0},{3,1},{4,6},{5,7},{6,4},{7,5},{8,10},{9,11},{10,... | collective-permute-start | bytes 245768 | tf_op jit(solution)/shard_map/ppermute | solution.py:269
  67.2 3.3 %collective-permute-start.2 = (bf16[80,512]{1,0:T(8,128)(2,1)}, bf16[80,512]{1,0:T(8,128)(2,1)S(1)}, u32[]{:S(2)}, u32[]{:S(2)}) collective-permute-start(bf16[80,512]{1,0:T(8,128)(2,1)} %get-tuple-element.18), channel_id=1, source_target_pairs={{0,3},{1,0},{2,1},{3,2},{4,7},{5,4},{6,5},{7,6},{8,11},{9,8},{10,9... | collective-permute-start | bytes 245768 | tf_op jit(solution)/shard_map/ppermute | solution.py:269
  70.4 0.0 all-to-all-done.1.parts_ref
  70.4 0.6 spread.1
  71.1 3.6 %all-to-all-start.2 = ((f32[4,4,128]{2,1,0:T(4,128)}), f32[4,4,128]{2,1,0:T(4,128)S(1)}, u32[]{:S(2)}, u32[]{:S(2)}) async-start(f32[4,4,128]{2,1,0:T(4,128)} %spread.1), calls=%async_computation.2 | async-start | bytes 16384 | tf_op jit(solution)/shard_map/all_to_all | solution.py:273
  74.6 0.0 collective-permute-done.refs_0_
  74.6 0.0 collective-permute-done.1.refs_1_
  74.6 0.0 collective-permute-done.2.refs_2_
  74.7 0.0 copy-done
  74.7 1.0 %cold_sum.1 = f32[128,512]{1,0:T(8,128)} custom-call(bf16[80,512]{1,0:T(8,128)(2,1)S(1)} %collective-permute-done.refs_0_, bf16[80,512]{1,0:T(8,128)(2,1)S(1)} %collective-permute-done.1.refs_1_, bf16[80,512]{1,0:T(8,128)(2,1)S(1)} %collective-permute-done.2.refs_2_, bf16[80,512]{1,0:T(8,128)(2,1)S(1)} %copy-done), custom_call_target="tpu_custom_call" | custom-call | flops 40000000 | bytes 600000 | tf_op jit(solution)/shard_map/cold_sum/pallas_call | solution.py:220
  75.7 4.3 %all-to-all-done.2 = f32[4,4,128]{2,1,0:T(4,128)S(1)} async-done(((f32[4,4,128]{2,1,0:T(4,128)}), f32[4,4,128]{2,1,0:T(4,128)S(1)}, u32[]{:S(2)}, u32[]{:S(2)}) %all-to-all-start.2) | async-done | bytes 8224 | tf_op jit(solution)/shard_map/all_to_all | solution.py:273
  80.0 0.6 copy.12
Async XLA Ops:
  8.6 66.1 %copy-start = (bf16[80,512]{1,0:T(8,128)(2,1)S(1)}, bf16[80,512]{1,0:T(8,128)(2,1)}, u32[]{:S(2)}) copy-start(bf16[80,512]{1,0:T(8,128)(2,1)} %get-tuple-element.19.refs_3_) | copy-start | bytes 245764
  8.6 20.6 %all-to-all-start = ((bf16[32,80,128]{2,1,0:T(8,128)(2,1)}), bf16[32,80,128]{2,1,0:T(8,128)(2,1)S(1)}, u32[]{:S(2)}, u32[]{:S(2)}) async-start(bf16[32,80,128]{2,1,0:T(8,128)(2,1)} %get-tuple-element.11), calls=%async_computation | async-start | bytes 1310720 | tf_op jit(solution)/shard_map/all_to_all | solution.py:261
  30.2 40.2 %all-to-all-start.1 = ((bf16[32,4,128]{2,1,0:T(4,128)(2,1)}), bf16[32,4,128]{2,1,0:T(4,128)(2,1)S(1)}, u32[]{:S(2)}, u32[]{:S(2)}) async-start(bf16[32,4,128]{2,1,0:T(4,128)(2,1)} %hot_sum.1), calls=%async_computation.1 | async-start | bytes 65536 | tf_op jit(solution)/shard_map/all_to_all | solution.py:267
  60.8 13.8 %collective-permute-start = (bf16[80,512]{1,0:T(8,128)(2,1)}, bf16[80,512]{1,0:T(8,128)(2,1)S(1)}, u32[]{:S(2)}, u32[]{:S(2)}) collective-permute-start(bf16[80,512]{1,0:T(8,128)(2,1)} %get-tuple-element.16), channel_id=1, source_target_pairs={{0,1},{1,2},{2,3},{3,0},{4,5},{5,6},{6,7},{7,4},{8,9},{9,10},{10,1... | collective-permute-start | bytes 245768 | tf_op jit(solution)/shard_map/ppermute | solution.py:269
  62.7 11.9 %collective-permute-start.1 = (bf16[80,512]{1,0:T(8,128)(2,1)}, bf16[80,512]{1,0:T(8,128)(2,1)S(1)}, u32[]{:S(2)}, u32[]{:S(2)}) collective-permute-start(bf16[80,512]{1,0:T(8,128)(2,1)} %get-tuple-element.17), channel_id=1, source_target_pairs={{0,2},{1,3},{2,0},{3,1},{4,6},{5,7},{6,4},{7,5},{8,10},{9,11},{10,... | collective-permute-start | bytes 245768 | tf_op jit(solution)/shard_map/ppermute | solution.py:269
  67.2 7.5 %collective-permute-start.2 = (bf16[80,512]{1,0:T(8,128)(2,1)}, bf16[80,512]{1,0:T(8,128)(2,1)S(1)}, u32[]{:S(2)}, u32[]{:S(2)}) collective-permute-start(bf16[80,512]{1,0:T(8,128)(2,1)} %get-tuple-element.18), channel_id=1, source_target_pairs={{0,3},{1,0},{2,1},{3,2},{4,7},{5,4},{6,5},{7,6},{8,11},{9,8},{10,9... | collective-permute-start | bytes 245768 | tf_op jit(solution)/shard_map/ppermute | solution.py:269
  71.1 8.9 %all-to-all-start.2 = ((f32[4,4,128]{2,1,0:T(4,128)}), f32[4,4,128]{2,1,0:T(4,128)S(1)}, u32[]{:S(2)}, u32[]{:S(2)}) async-start(f32[4,4,128]{2,1,0:T(4,128)} %spread.1), calls=%async_computation.2 | async-start | bytes 16384 | tf_op jit(solution)/shard_map/all_to_all | solution.py:273

commit v6 on v5

--- a/solution.py
+++ b/solution.py
@@ -146,7 +146,7 @@
         else:
             piece = width // owners
             for block in range(out.shape[0]):
-                start = block % owners * piece
+                start = (block + 1) % owners * piece
                 out[block, :CAP, :] = sent[:, start : start + piece]
                 out[block, CAP:, :] = slot_ids
 
@@ -270,7 +270,8 @@
         for step, rows in enumerate(sent, start=1)
     ]
     cold_grad = cold_call([*received, own_rows])
-    copies = lax.all_to_all(spread_call(owners, parts), "table", 0, 0)
+    last = [(owners - 1 + i) % owners for i in range(owners)]
+    copies = lax.all_to_all(spread_call(owners, parts), "table", 0, 0, axis_index_groups=[last])
     hot_grad = jnp.transpose(copies, (1, 0, 2)).reshape(HOT_DEV, width)
     return (hot_grad, cold_grad)
 

time: 81 us -> 80 us (0.988)
  waiting for transfers between devices: 17.4 us -> 15.3 us
  starting transfers between devices: 51.2 us -> 52.3 us
    all_to_all x1, waiting for transfers between devices: 4.3 us -> 2.25 us  [shards(): lax.all_to_all(spread_call(owners, parts), 'table', 0, 0, axis_index_grou...]
    all_to_all x1, starting transfers between devices: 3.57 us -> 4.61 us  [shards(): lax.all_to_all(spread_call(owners, parts), 'table', 0, 0, axis_index_grou...]
where the time goes in v6:
time: 80 us; the launch traced here: 79.5 us
  starting transfers between devices  52.3 us (65%)
  waiting for transfers between devices  15.3 us (19%)
  Pallas kernels  9.92 us (12%)
  between operations  1.37 us (2%)
    all_to_all x1, starting transfers between devices, shards(): parts = lax.all_to_all(partial, 'z', 0, 0, axis_index_groups=[order])  30.6 us
    all_to_all x1, waiting for transfers between devices, shards(): gathered = lax.all_to_all(hot_rows, ('y', 'core', 'table'), 0, 0)  13.1 us
    ppermute x3, starting transfers between devices, shards(): lax.ppermute(rows, 'table', [(i, (i + step) % owners) for i in range(owne...  9.58 us
    all_to_all x1, starting transfers between devices, shards(): gathered = lax.all_to_all(hot_rows, ('y', 'core', 'table'), 0, 0)  7.47 us
    pallas_call x1, Pallas kernels, item_call(): pl.pallas_call(functools.partial(item_kernel, owners), in_specs=[pl.Block...  7.27 us
    all_to_all x1, starting transfers between devices, shards(): lax.all_to_all(spread_call(owners, parts), 'table', 0, 0, axis_index_grou...  4.61 us
    all_to_all x1, waiting for transfers between devices, shards(): lax.all_to_all(spread_call(owners, parts), 'table', 0, 0, axis_index_grou...  2.25 us
  transfers between devices with their start and end apart: 6, of which 2 were waited for; matrix products, arithmetic and copies ran while one was open for 0% of the time, Pallas kernels for 2%

profile of v6, /device:TPU:32, one launch (start us, length us, event | category | flops | bytes accessed | tf_op | source)
XLA Modules:
  0.0 79.5 jit_solution(14755410042144236669)
XLA Ops:
  1.3 7.3 %item_grad.1 = (bf16[80,512]{1,0:T(8,128)(2,1)}, bf16[80,512]{1,0:T(8,128)(2,1)}, bf16[80,512]{1,0:T(8,128)(2,1)}, bf16[80,512]{1,0:T(8,128)(2,1)}, bf16[32,80,128]{2,1,0:T(8,128)(2,1)}) custom-call(s32[1]{0:T(128)S(6)} %copy.11.refs_0_, s32[1]{0:T(128)} %bitcast.1.refs_1_, bf16[192,512]{1,0:T(8,128)(2,1)} %bitcast.9, bf16[192,512]{1,0:T(8,128)(2,1)} %bitcast.10, ...), custom_call_target="tpu_custom_call" | custom-call | flops 1200000000 | bytes 4500000 | tf_op jit(solution)/shard_map/item_grad/pallas_call | solution.py:159
  8.6 0.0 copy-start
  8.6 7.5 %all-to-all-start = ((bf16[32,80,128]{2,1,0:T(8,128)(2,1)}), bf16[32,80,128]{2,1,0:T(8,128)(2,1)S(1)}, u32[]{:S(2)}, u32[]{:S(2)}) async-start(bf16[32,80,128]{2,1,0:T(8,128)(2,1)} %get-tuple-element.11), calls=%async_computation | async-start | bytes 1310720 | tf_op jit(solution)/shard_map/all_to_all | solution.py:261
  16.1 13.1 %all-to-all-done.rows_ref = bf16[32,80,128]{2,1,0:T(8,128)(2,1)S(1)} async-done(((bf16[32,80,128]{2,1,0:T(8,128)(2,1)}), bf16[32,80,128]{2,1,0:T(8,128)(2,1)S(1)}, u32[]{:S(2)}, u32[]{:S(2)}) %all-to-all-start) | async-done | bytes 655392 | tf_op jit(solution)/shard_map/all_to_all | solution.py:261
  29.1 1.0 %hot_sum.1 = bf16[32,4,128]{2,1,0:T(4,128)(2,1)} custom-call(s32[1]{0:T(128)} %bitcast.base_ref, bf16[32,80,128]{2,1,0:T(8,128)(2,1)S(1)} %all-to-all-done.rows_ref), custom_call_target="tpu_custom_call" | custom-call | flops 80000000 | bytes 800000 | tf_op jit(solution)/shard_map/hot_sum/pallas_call | solution.py:203
  30.2 30.6 %all-to-all-start.1 = ((bf16[32,4,128]{2,1,0:T(4,128)(2,1)}), bf16[32,4,128]{2,1,0:T(4,128)(2,1)S(1)}, u32[]{:S(2)}, u32[]{:S(2)}) async-start(bf16[32,4,128]{2,1,0:T(4,128)(2,1)} %hot_sum.1), calls=%async_computation.1 | async-start | bytes 65536 | tf_op jit(solution)/shard_map/all_to_all | solution.py:267
  60.8 1.9 %collective-permute-start = (bf16[80,512]{1,0:T(8,128)(2,1)}, bf16[80,512]{1,0:T(8,128)(2,1)S(1)}, u32[]{:S(2)}, u32[]{:S(2)}) collective-permute-start(bf16[80,512]{1,0:T(8,128)(2,1)} %get-tuple-element.16), channel_id=1, source_target_pairs={{0,1},{1,2},{2,3},{3,0},{4,5},{5,6},{6,7},{7,4},{8,9},{9,10},{10,1... | collective-permute-start | bytes 245768 | tf_op jit(solution)/shard_map/ppermute | solution.py:269
  62.7 4.4 %collective-permute-start.1 = (bf16[80,512]{1,0:T(8,128)(2,1)}, bf16[80,512]{1,0:T(8,128)(2,1)S(1)}, u32[]{:S(2)}, u32[]{:S(2)}) collective-permute-start(bf16[80,512]{1,0:T(8,128)(2,1)} %get-tuple-element.17), channel_id=1, source_target_pairs={{0,2},{1,3},{2,0},{3,1},{4,6},{5,7},{6,4},{7,5},{8,10},{9,11},{10,... | collective-permute-start | bytes 245768 | tf_op jit(solution)/shard_map/ppermute | solution.py:269
  67.2 3.3 %collective-permute-start.2 = (bf16[80,512]{1,0:T(8,128)(2,1)}, bf16[80,512]{1,0:T(8,128)(2,1)S(1)}, u32[]{:S(2)}, u32[]{:S(2)}) collective-permute-start(bf16[80,512]{1,0:T(8,128)(2,1)} %get-tuple-element.18), channel_id=1, source_target_pairs={{0,3},{1,0},{2,1},{3,2},{4,7},{5,4},{6,5},{7,6},{8,11},{9,8},{10,9... | collective-permute-start | bytes 245768 | tf_op jit(solution)/shard_map/ppermute | solution.py:269
  70.4 0.0 all-to-all-done.1.parts_ref
  70.4 0.6 spread.1
  71.1 4.6 %all-to-all-start.2 = ((f32[4,4,128]{2,1,0:T(4,128)}), f32[4,4,128]{2,1,0:T(4,128)S(1)}, u32[]{:S(2)}, u32[]{:S(2)}) async-start(f32[4,4,128]{2,1,0:T(4,128)} %spread.1), calls=%async_computation.2 | async-start | bytes 16384 | tf_op jit(solution)/shard_map/all_to_all | solution.py:274
  75.7 0.0 collective-permute-done.refs_0_
  75.7 0.0 collective-permute-done.1.refs_1_
  75.7 0.0 collective-permute-done.2.refs_2_
  75.7 0.0 copy-done
  75.7 1.0 %cold_sum.1 = f32[128,512]{1,0:T(8,128)} custom-call(bf16[80,512]{1,0:T(8,128)(2,1)S(1)} %collective-permute-done.refs_0_, bf16[80,512]{1,0:T(8,128)(2,1)S(1)} %collective-permute-done.1.refs_1_, bf16[80,512]{1,0:T(8,128)(2,1)S(1)} %collective-permute-done.2.refs_2_, bf16[80,512]{1,0:T(8,128)(2,1)S(1)} %copy-done), custom_call_target="tpu_custom_call" | custom-call | flops 40000000 | bytes 600000 | tf_op jit(solution)/shard_map/cold_sum/pallas_call | solution.py:220
  76.7 2.2 %all-to-all-done.2 = f32[4,4,128]{2,1,0:T(4,128)S(1)} async-done(((f32[4,4,128]{2,1,0:T(4,128)}), f32[4,4,128]{2,1,0:T(4,128)S(1)}, u32[]{:S(2)}, u32[]{:S(2)}) %all-to-all-start.2) | async-done | bytes 8224 | tf_op jit(solution)/shard_map/all_to_all | solution.py:274
  78.9 0.6 copy.12
Async XLA Ops:
  8.6 67.1 %copy-start = (bf16[80,512]{1,0:T(8,128)(2,1)S(1)}, bf16[80,512]{1,0:T(8,128)(2,1)}, u32[]{:S(2)}) copy-start(bf16[80,512]{1,0:T(8,128)(2,1)} %get-tuple-element.19.refs_3_) | copy-start | bytes 245764
  8.6 20.6 %all-to-all-start = ((bf16[32,80,128]{2,1,0:T(8,128)(2,1)}), bf16[32,80,128]{2,1,0:T(8,128)(2,1)S(1)}, u32[]{:S(2)}, u32[]{:S(2)}) async-start(bf16[32,80,128]{2,1,0:T(8,128)(2,1)} %get-tuple-element.11), calls=%async_computation | async-start | bytes 1310720 | tf_op jit(solution)/shard_map/all_to_all | solution.py:261
  30.2 40.2 %all-to-all-start.1 = ((bf16[32,4,128]{2,1,0:T(4,128)(2,1)}), bf16[32,4,128]{2,1,0:T(4,128)(2,1)S(1)}, u32[]{:S(2)}, u32[]{:S(2)}) async-start(bf16[32,4,128]{2,1,0:T(4,128)(2,1)} %hot_sum.1), calls=%async_computation.1 | async-start | bytes 65536 | tf_op jit(solution)/shard_map/all_to_all | solution.py:267
  60.8 14.9 %collective-permute-start = (bf16[80,512]{1,0:T(8,128)(2,1)}, bf16[80,512]{1,0:T(8,128)(2,1)S(1)}, u32[]{:S(2)}, u32[]{:S(2)}) collective-permute-start(bf16[80,512]{1,0:T(8,128)(2,1)} %get-tuple-element.16), channel_id=1, source_target_pairs={{0,1},{1,2},{2,3},{3,0},{4,5},{5,6},{6,7},{7,4},{8,9},{9,10},{10,1... | collective-permute-start | bytes 245768 | tf_op jit(solution)/shard_map/ppermute | solution.py:269
  62.7 12.9 %collective-permute-start.1 = (bf16[80,512]{1,0:T(8,128)(2,1)}, bf16[80,512]{1,0:T(8,128)(2,1)S(1)}, u32[]{:S(2)}, u32[]{:S(2)}) collective-permute-start(bf16[80,512]{1,0:T(8,128)(2,1)} %get-tuple-element.17), channel_id=1, source_target_pairs={{0,2},{1,3},{2,0},{3,1},{4,6},{5,7},{6,4},{7,5},{8,10},{9,11},{10,... | collective-permute-start | bytes 245768 | tf_op jit(solution)/shard_map/ppermute | solution.py:269
  67.2 8.5 %collective-permute-start.2 = (bf16[80,512]{1,0:T(8,128)(2,1)}, bf16[80,512]{1,0:T(8,128)(2,1)S(1)}, u32[]{:S(2)}, u32[]{:S(2)}) collective-permute-start(bf16[80,512]{1,0:T(8,128)(2,1)} %get-tuple-element.18), channel_id=1, source_target_pairs={{0,3},{1,0},{2,1},{3,2},{4,7},{5,4},{6,5},{7,6},{8,11},{9,8},{10,9... | collective-permute-start | bytes 245768 | tf_op jit(solution)/shard_map/ppermute | solution.py:269
  71.1 7.9 %all-to-all-start.2 = ((f32[4,4,128]{2,1,0:T(4,128)}), f32[4,4,128]{2,1,0:T(4,128)S(1)}, u32[]{:S(2)}, u32[]{:S(2)}) async-start(f32[4,4,128]{2,1,0:T(4,128)} %spread.1), calls=%async_computation.2 | async-start | bytes 16384 | tf_op jit(solution)/shard_map/all_to_all | solution.py:274
